TPU v7x, 128 devices: a whole 4x4x4 slice. The times are simulated.
128 devices in a mesh: blk: 32 (over x, y, core), cross: 4 (over z).
Axes of the slice: x: 4, y: 4, z: 4, core: 2. Of those that a mesh axis runs over, the one named last changes fastest.
Arguments:
- base_column: int32 [32768], P(('blk', 'cross')), may hold values from 0 to 511
- base_zbin: int32 [32768, 128], P(('blk', 'cross')), may hold values from 0 to 1023
- base_frac: float32 [3, 32768, 128], P(None, ('blk', 'cross')), may hold values from 0 to 1
- base_weight: float32 [32768, 128], P(('blk', 'cross')), may hold values from 0.25 to 4
- fine_column: int32 [114688], P(('blk', 'cross')), may hold values from 0 to 224
- fine_zbin: int32 [114688, 128], P(('blk', 'cross')), may hold values from 0 to 62
- fine_frac: float32 [3, 114688, 128], P(None, ('blk', 'cross')), may hold values from 0 to 1
- fine_weight: float32 [114688, 128], P(('blk', 'cross')), may hold values from 0.25 to 4
- tile_box: int32 [114688], P(('blk', 'cross')), may hold values from 0 to 1023, as said below
- box_home: int32 [1024], replicated, may hold values from 0 to 127, as said below
- box_anchor: int32 [1024], replicated, may hold values from 0 to 255, as said below
Outputs:
- base_mass: float32 [256, 256, 1024], P('blk', 'cross')
- fine_mass: float32 [1024, 16384], P(('blk', 'cross'))
Inputs may be any that keep to these rules, and one draw needn't show every extreme that they name: `box_home`: box r is owned by device r // 8; every device is home to exactly 8 boxes, and the 8 boxes of one owner have distinct homes. `box_anchor`: boxes with the same home have distinct positions. `tile_box`: the tiles of one device are sorted by the owner of their box; every device holds 16 tiles of the boxes of each owner of a quarter of the owners, and 4 of each of the others.
All inputs are finite; a program needn't handle non-finite values.
Results may differ from a plain program's by a relative error of at most 0.0003.
Values sent between devices are 32-bit elements; how exact they have to be, the bound alone decides.
No kernel may reach another device: no remote copies, remote signals or barrier semaphores. Data moves between devices by JAX's collectives and lax.ppermute only.
A program may use at most 192 MiB of HBM per device.

v0:
```python
import math

import jax
import jax.numpy as jnp
from jax import lax
from jax.sharding import PartitionSpec as P

CX = 8
CY = 64
NZ = 1024
BX = 8
BY = 8
BZ = 32
BPH = 8
CAP = 16


highest_precision = lax.Precision.HIGHEST


def shifted(value, axis, steps):
    count = lax.axis_size(axis)
    pairs = [(source, (source + steps) % count) for source in range(count)]
    return lax.ppermute(value, axis, pairs)


def corner_rows(fractions, masses):
    along_x, along_y, along_z = (fractions[0], fractions[1], fractions[2])
    result = []
    for first in (0, 1):
        for second in (0, 1):
            for third in (0, 1):
                part_x = along_x if first else 1.0 - along_x
                part_y = along_y if second else 1.0 - along_y
                part_z = along_z if third else 1.0 - along_z
                result.append(masses * part_x * part_y * part_z)
    return jnp.stack(result, axis=1)


def block_profiles(zbins, fractions, masses, length, lower):
    upper = length // lower
    weights = corner_rows(fractions, masses)
    upper_hot = (zbins[:, :, None] // lower == jnp.arange(upper, dtype=jnp.int32)).astype(
        jnp.float32
    )
    lower_hot = (zbins[:, :, None] % lower == jnp.arange(lower, dtype=jnp.int32)).astype(
        jnp.float32
    )
    mixed = weights[:, :, None, :] * jnp.swapaxes(upper_hot, 1, 2)[:, None, :, :]
    mixed = mixed.reshape(weights.shape[0], 8 * upper, weights.shape[2])
    spread = jnp.einsum("tmp,tpl->tml", mixed, lower_hot, precision=highest_precision)
    spread = spread.reshape(weights.shape[0], 4, 2, length)
    return spread[:, :, 0] + jnp.roll(spread[:, :, 1], 1, axis=2)


def tile_profiles(zbins, fractions, masses, length, lower):
    count = zbins.shape[0]
    group = math.gcd(count, 256)
    steps = count // group
    zbins_g = zbins.reshape(steps, group, zbins.shape[1])
    fractions_g = jnp.swapaxes(fractions.reshape(3, steps, group, zbins.shape[1]), 0, 1)
    masses_g = masses.reshape(steps, group, zbins.shape[1])

    def tile_one_group(pieces):
        return block_profiles(pieces[0], pieces[1], pieces[2], length, lower)

    result = lax.map(tile_one_group, (zbins_g, fractions_g, masses_g))
    return result.reshape(count, 4, length)


def column_sums(columns, zbins, fractions, masses):
    count = zbins.shape[0]
    group = math.gcd(count, 256)
    steps = count // group
    columns_g = columns.reshape(steps, group)
    zbins_g = zbins.reshape(steps, group, zbins.shape[1])
    fractions_g = jnp.swapaxes(fractions.reshape(3, steps, group, zbins.shape[1]), 0, 1)
    masses_g = masses.reshape(steps, group, zbins.shape[1])

    def column_one_group(total, pieces):
        profile = block_profiles(pieces[1], pieces[2], pieces[3], NZ, 16)
        column_hot = (pieces[0][:, None] == jnp.arange(CX * CY, dtype=jnp.int32)[None, :]).astype(
            jnp.float32
        )
        added = jnp.dot(
            column_hot.T,
            profile.reshape(group, 4 * NZ),
            precision=highest_precision,
            preferred_element_type=jnp.float32,
        )
        return (total + added, 0)

    start = jnp.zeros((CX * CY, 4 * NZ), jnp.float32)
    summed, _ = lax.scan(column_one_group, start, (columns_g, zbins_g, fractions_g, masses_g))
    return summed


def shards(
    base_column,
    base_zbin,
    base_frac,
    base_weight,
    fine_column,
    fine_zbin,
    fine_frac,
    fine_weight,
    tile_box,
    box_home,
    box_anchor,
):
    nodes = lax.axis_size(("blk", "cross"))
    myself = lax.axis_index(("blk", "cross"))
    fine_len = 2 * BZ
    stride = 2 * BY - 1
    start_columns = (2 * BX - 1) * stride
    fine_columns = 4 * BX * BY
    coarse = BX * BY * BZ
    summed = column_sums(base_column, base_zbin, base_frac, base_weight)
    summed = summed.reshape(CX, CY, 4, NZ)
    grid = jnp.zeros((CX + 1, CY + 1, NZ), jnp.float32)
    for first in (0, 1):
        for second in (0, 1):
            grid = grid + jnp.pad(
                summed[:, :, 2 * first + second], ((first, 1 - first), (second, 1 - second), (0, 0))
            )
    incoming = shifted(grid[CX], "blk", 1)
    core = grid[:CX].at[0].add(incoming)
    beside = shifted(core[:, CY], "cross", 1)
    core = core[:, :CY].at[:, 0].add(beside)
    fine_prof = tile_profiles(fine_zbin, fine_frac, fine_weight, fine_len, 8)
    tiles = fine_prof.shape[0]
    owners = tile_box // BPH
    owner_hot = (owners[:, None] == jnp.arange(nodes, dtype=jnp.int32)).astype(jnp.int32)
    counts = jnp.sum(owner_hot, axis=0)
    firsts = jnp.cumsum(counts) - counts
    slots = jnp.arange(tiles, dtype=jnp.int32) - jnp.sum(owner_hot * firsts[None, :], axis=1)
    labels = (tile_box % BPH * start_columns + fine_column).astype(jnp.float32)
    destination = owners * CAP + slots
    slot_hot = (destination[:, None] == jnp.arange(nodes * CAP, dtype=jnp.int32)[None, :]).astype(
        jnp.float32
    )
    outgoing = jnp.dot(
        slot_hot.T,
        fine_prof.reshape(tiles, 4 * fine_len),
        precision=highest_precision,
        preferred_element_type=jnp.float32,
    ).reshape(nodes, CAP, 4 * fine_len)
    header = jnp.dot(
        labels, slot_hot, precision=highest_precision, preferred_element_type=jnp.float32
    ).reshape(nodes, CAP)
    arrived, places = (
        lax.all_to_all(outgoing, ("blk", "cross"), split_axis=0, concat_axis=0, tiled=True),
        lax.all_to_all(header, ("blk", "cross"), split_axis=0, concat_axis=0, tiled=True),
    )
    place_int = places.reshape(-1).astype(jnp.int32)
    local_box = place_int // start_columns
    column = place_int % start_columns
    column_x = column // stride
    column_y = column % stride
    arrived_rows = arrived.reshape(-1, 4, fine_len)
    row_ids = jnp.arange(BPH * fine_columns, dtype=jnp.int32)[None, :]
    fine_rows = jnp.zeros((BPH * fine_columns, fine_len), jnp.float32)
    for first in (0, 1):
        for second in (0, 1):
            target = local_box * fine_columns + (column_x + first) * (2 * BY) + column_y + second
            target_hot = (target[:, None] == row_ids).astype(jnp.float32)
            fine_rows = fine_rows + jnp.dot(
                target_hot.T,
                arrived_rows[:, 2 * first + second],
                precision=highest_precision,
                preferred_element_type=jnp.float32,
            )
    fine_rows = fine_rows.reshape(BPH, fine_columns * fine_len)
    reduced = fine_rows.reshape(BPH, BX, 2, BY, 2, BZ, 2).sum(axis=(2, 4, 6)).reshape(BPH, coarse)
    my_homes = lax.dynamic_slice_in_dim(box_home, myself * BPH, BPH, 0)
    sending = jnp.zeros((nodes, coarse), jnp.float32).at[my_homes].set(reduced)
    returned = lax.all_to_all(sending, ("blk", "cross"), split_axis=0, concat_axis=0, tiled=True)
    match = box_home.reshape(nodes, BPH) == myself
    present = jnp.any(match, axis=1).astype(jnp.float32)
    anchors = jnp.sum(jnp.where(match, box_anchor.reshape(nodes, BPH), 0), axis=1)
    lattice = (
        core.reshape(CX // BX, BX, CY // BY, BY, NZ // BZ, BZ)
        .transpose(0, 2, 4, 1, 3, 5)
        .reshape(-1, coarse)
    )
    lattice = lattice.at[anchors].add(returned * present[:, None])
    base_out = (
        lattice.reshape(CX // BX, CY // BY, NZ // BZ, BX, BY, BZ)
        .transpose(0, 3, 1, 4, 2, 5)
        .reshape(CX, CY, NZ)
    )
    return (base_out, fine_rows)


def solution(mesh):
    placed = (
        P(("blk", "cross")),
        P(("blk", "cross"), None),
        P(None, ("blk", "cross"), None),
        P(("blk", "cross"), None),
        P(("blk", "cross")),
        P(("blk", "cross"), None),
        P(None, ("blk", "cross"), None),
        P(("blk", "cross"), None),
        P(("blk", "cross")),
        P(),
        P(),
    )
    return jax.shard_map(
        shards,
        mesh=mesh,
        in_specs=placed,
        out_specs=(P("blk", "cross", None), P(("blk", "cross"), None)),
        check_vma=False,
    )
```

profile of v0, /device:TPU:1, one launch (start us, length us, event | category | flops | bytes accessed | tf_op | source)
XLA Modules:
  0.0 416.4 jit_solution(76004318771440650)
XLA Ops:
  3.1 2.4 fusion.24
  6.3 12.7 %all-to-all-start = ((f32[128,1,16]{2,1,0:T(1,128)}), f32[128,1,16]{2,1,0:T(1,128)}, u32[]{:S(2)}, u32[]{:S(2)}) async-start(f32[128,1,16]{2,1,0:T(1,128)} %bitcast.45), calls=%async_computation | async-start | bytes 131072 | tf_op jit(solution)/shard_map/all_to_all | solution.py:153
  24.2 21.5 %broadcast_multiply_fusion = f32[256,8,64,128]{3,2,1,0:T(8,128)} fusion(f32[256,64,128]{2,1,0:T(8,128)S(1)} %fusion.21, f32[256,8,128]{2,1,0:T(8,128)S(1)} %copy.104), kind=kLoop, calls=%fused_computation.44 | loop fusion | flops 16777216 | bytes 76546048 | tf_op jit(solution)/shard_map/while/body/eval_jaxpr/mul | solution.py:49
  45.7 35.9 %fusion.29 = f32[256,512,16]{1,2,0:T(8,128)} fusion(f32[256,512,128]{2,1,0:T(8,128)} %bitcast.25, s32[256,128]{1,0:T(8,128)S(1)} %get-tuple-element.174), kind=kOutput, calls=%fused_computation.78 | convolution fusion | flops 3221749760 | bytes 75628544 | tf_op jit(solution)/shard_map/while/body/eval_jaxpr/tmp,tpl->tml/dot_general | solution.py:51
  81.5 10.5 %copy.105 = f32[256,512,16]{0,2,1:T(8,128)} copy(f32[256,512,16]{1,2,0:T(8,128)} %fusion.29) | data formatting | bytes 16777216 | tf_op jit(solution)/shard_map/while/body/eval_jaxpr/tmp,tpl->tml/dot_general | solution.py:51
  92.0 6.0 %fusion.56 = (f32[256,4,1,1024]{0,3,2,1:T(8,128)}, f32[256,4,1024]{0,2,1:T(8,128)S(1)}) fusion(f32[256,4,2,1024]{0,3,2,1:T(8,128)} %bitcast.316), kind=kLoop, calls=%fused_computation.162 | loop fusion | bytes 16777216 | tf_op jit(solution)/shard_map/while/body/eval_jaxpr/slice | solution.py:53
  98.0 1.9 copy-done.4
  101.1 91.8 %while.18 = (s32[]{:T(128)}, f32[7,128,4,64]{1,0,3,2:T(8,128)}, f32[7,128,128]{2,1,0:T(8,128)}, f32[7,3,128,128]{3,2,0,1:T(8,128)}, s32[7,128,128]{2,1,0:T(8,128)}, /*index=5*/s32[]{:T(128)}, s32[]{:T(128)}) while((s32[]{:T(128)}, f32[7,128,4,64]{1,0,3,2:T(8,128)}, f32[7,128,128]{2,1,0:T(8,128)}, f32[7,3,128,128]{3,2,0,1:T(8,128)}, ...), condition=%wide.region_5.6_spmd, body=%wide.region_4.5_spmd.sunk | while | flops 103022592 | bytes 7766117 | solution.py:67
  106.1 3.4 fusion.73
  109.8 4.4 %dynamic_update_slice.8 = f32[7,128,4,64]{1,0,3,2:T(8,128)} dynamic-update-slice(f32[7,128,4,64]{1,0,3,2:T(8,128)} %get-tuple-element.231, f32[1,128,4,64]{1,0,3,2:T(1,128)S(1)} %bitcast.321, s32[]{:T(128)} %get-tuple-element.230, s32[]{:T(128)} %constant.235.clone.1..sunk, s32[]{:T(128)} %constant.235.clone.1..sunk, s32[]{:T(128)} %constant.235.clone.1..sunk) | dynamic-update-slice | bytes 262148 | tf_op jit(solution)/shard_map/while/body/jit(dynamic_update_index_in_dim)/dynamic_update_slice | solution.py:67
  119.2 3.4 fusion.73
  122.9 4.4 %dynamic_update_slice.8 = f32[7,128,4,64]{1,0,3,2:T(8,128)} dynamic-update-slice(f32[7,128,4,64]{1,0,3,2:T(8,128)} %get-tuple-element.231, f32[1,128,4,64]{1,0,3,2:T(1,128)S(1)} %bitcast.321, s32[]{:T(128)} %get-tuple-element.230, s32[]{:T(128)} %constant.235.clone.1..sunk, s32[]{:T(128)} %constant.235.clone.1..sunk, s32[]{:T(128)} %constant.235.clone.1..sunk) | dynamic-update-slice | bytes 262148 | tf_op jit(solution)/shard_map/while/body/jit(dynamic_update_index_in_dim)/dynamic_update_slice | solution.py:67
  132.3 3.4 fusion.73
  136.0 4.4 %dynamic_update_slice.8 = f32[7,128,4,64]{1,0,3,2:T(8,128)} dynamic-update-slice(f32[7,128,4,64]{1,0,3,2:T(8,128)} %get-tuple-element.231, f32[1,128,4,64]{1,0,3,2:T(1,128)S(1)} %bitcast.321, s32[]{:T(128)} %get-tuple-element.230, s32[]{:T(128)} %constant.235.clone.1..sunk, s32[]{:T(128)} %constant.235.clone.1..sunk, s32[]{:T(128)} %constant.235.clone.1..sunk) | dynamic-update-slice | bytes 262148 | tf_op jit(solution)/shard_map/while/body/jit(dynamic_update_index_in_dim)/dynamic_update_slice | solution.py:67
  145.4 3.4 fusion.73
  149.1 4.4 %dynamic_update_slice.8 = f32[7,128,4,64]{1,0,3,2:T(8,128)} dynamic-update-slice(f32[7,128,4,64]{1,0,3,2:T(8,128)} %get-tuple-element.231, f32[1,128,4,64]{1,0,3,2:T(1,128)S(1)} %bitcast.321, s32[]{:T(128)} %get-tuple-element.230, s32[]{:T(128)} %constant.235.clone.1..sunk, s32[]{:T(128)} %constant.235.clone.1..sunk, s32[]{:T(128)} %constant.235.clone.1..sunk) | dynamic-update-slice | bytes 262148 | tf_op jit(solution)/shard_map/while/body/jit(dynamic_update_index_in_dim)/dynamic_update_slice | solution.py:67
  158.5 3.4 fusion.73
  162.1 4.4 %dynamic_update_slice.8 = f32[7,128,4,64]{1,0,3,2:T(8,128)} dynamic-update-slice(f32[7,128,4,64]{1,0,3,2:T(8,128)} %get-tuple-element.231, f32[1,128,4,64]{1,0,3,2:T(1,128)S(1)} %bitcast.321, s32[]{:T(128)} %get-tuple-element.230, s32[]{:T(128)} %constant.235.clone.1..sunk, s32[]{:T(128)} %constant.235.clone.1..sunk, s32[]{:T(128)} %constant.235.clone.1..sunk) | dynamic-update-slice | bytes 262148 | tf_op jit(solution)/shard_map/while/body/jit(dynamic_update_index_in_dim)/dynamic_update_slice | solution.py:67
  171.6 3.4 fusion.73
  175.2 4.4 %dynamic_update_slice.8 = f32[7,128,4,64]{1,0,3,2:T(8,128)} dynamic-update-slice(f32[7,128,4,64]{1,0,3,2:T(8,128)} %get-tuple-element.231, f32[1,128,4,64]{1,0,3,2:T(1,128)S(1)} %bitcast.321, s32[]{:T(128)} %get-tuple-element.230, s32[]{:T(128)} %constant.235.clone.1..sunk, s32[]{:T(128)} %constant.235.clone.1..sunk, s32[]{:T(128)} %constant.235.clone.1..sunk) | dynamic-update-slice | bytes 262148 | tf_op jit(solution)/shard_map/while/body/jit(dynamic_update_index_in_dim)/dynamic_update_slice | solution.py:67
  184.6 3.4 fusion.73
  188.3 4.4 %dynamic_update_slice.8 = f32[7,128,4,64]{1,0,3,2:T(8,128)} dynamic-update-slice(f32[7,128,4,64]{1,0,3,2:T(8,128)} %get-tuple-element.231, f32[1,128,4,64]{1,0,3,2:T(1,128)S(1)} %bitcast.321, s32[]{:T(128)} %get-tuple-element.230, s32[]{:T(128)} %constant.235.clone.1..sunk, s32[]{:T(128)} %constant.235.clone.1..sunk, s32[]{:T(128)} %constant.235.clone.1..sunk) | dynamic-update-slice | bytes 262148 | tf_op jit(solution)/shard_map/while/body/jit(dynamic_update_index_in_dim)/dynamic_update_slice | solution.py:67
  194.4 2.8 pad_maximum_fusion
  197.8 3.0 bitcast_add_fusion
  200.8 6.7 %fusion.22 = f32[128,16,256]{2,1,0:T(8,128)} fusion(f32[896,256,1]{0,1,2:T(8,128)S(1)} %reshape.832, pred[128,16,896]{2,0,1:T(32,128)(4,1)S(1)} %broadcast_compare_fusion), kind=kOutput, calls=%fused_computation.61 | convolution fusion | flops 5637144576 | bytes 4849664 | tf_op jit(solution)/shard_map/dot_general | solution.py:142
  207.5 10.2 %all-to-all-start.1 = ((f32[128,16,256]{2,1,0:T(8,128)}), f32[128,16,256]{2,1,0:T(8,128)}, u32[]{:S(2)}, u32[]{:S(2)}) async-start(f32[128,16,256]{2,1,0:T(8,128)} %fusion.22), calls=%async_computation.1 | async-start | bytes 4194304 | tf_op jit(solution)/shard_map/all_to_all | solution.py:152
  217.7 6.0 %fusion.36 = f32[8,64,4,1024]{3,1,2,0:T(8,128)S(1)} fusion(f32[4,1024,256,1]{2,1,0,3:T(8,128)} %bitcast.320, s32[8,64]{1,0:T(8,128)S(1)} %multiply_add_fusion.1, s32[256]{0:T(256)S(1)} %copy-done.9), kind=kOutput, calls=%fused_computation.86 | convolution fusion | flops 6442582016 | bytes 12585984 | tf_op jit(solution)/shard_map/while/body/eval_jaxpr/dot_general | solution.py:85
  232.6 16.0 %all-to-all-done.1 = f32[128,16,256]{2,1,0:T(8,128)} async-done(((f32[128,16,256]{2,1,0:T(8,128)}), f32[128,16,256]{2,1,0:T(8,128)}, u32[]{:S(2)}, u32[]{:S(2)}) %all-to-all-start.1) | async-done | bytes 2097184 | tf_op jit(solution)/shard_map/all_to_all | solution.py:152
  248.6 5.1 %reshape.803 = f32[2048,4,64]{2,1,0:T(4,128)} reshape(f32[128,16,256]{2,1,0:T(8,128)} %all-to-all-done.1) | data formatting | bytes 4194304 | tf_op jit(solution)/shard_map/reshape | solution.py:160
  253.7 11.0 %fusion.57 = (f32[2048,1,64]{2,1,0:T(1,128)S(1)}, f32[2048,1,64]{2,1,0:T(1,128)S(1)}, f32[2048,1,64]{2,1,0:T(1,128)S(1)}, f32[2048,1,64]{2,1,0:T(1,128)S(1)}) fusion(f32[2048,4,64]{2,1,0:T(4,128)} %reshape.803), kind=kLoop, calls=%fused_computation.163 | loop fusion | bytes 4194304 | tf_op jit(solution)/shard_map/slice | solution.py:169
  264.7 6.5 %fusion.13 = f32[2048,64]{0,1:T(8,128)S(1)} fusion(f32[2048,64]{1,0:T(8,128)S(1)} %bitcast.325, s32[2048]{0:T(1024)S(1)} %get-tuple-element.177), kind=kOutput, calls=%fused_computation.49 | convolution fusion | flops 3225419776 | bytes 1056768 | tf_op jit(solution)/shard_map/dot_general | solution.py:167
  271.2 6.5 %fusion.28 = f32[2048,64]{0,1:T(8,128)S(1)} fusion(f32[2048,64]{0,1:T(8,128)S(1)} %fusion.13, f32[2048,64]{1,0:T(8,128)S(1)} %bitcast.324, s32[2048]{0:T(1024)S(1)} %get-tuple-element.176), kind=kOutput, calls=%fused_computation.72 | convolution fusion | flops 3225550848 | bytes 1581056 | tf_op jit(solution)/shard_map/dot_general | solution.py:167
  277.7 6.7 %fusion.27 = f32[2048,64]{0,1:T(8,128)S(1)} fusion(f32[2048,64]{0,1:T(8,128)S(1)} %fusion.28, f32[2048,64]{1,0:T(8,128)S(1)} %bitcast.323, s32[2048]{0:T(1024)S(1)} %get-tuple-element.157), kind=kOutput, calls=%fused_computation.71 | convolution fusion | flops 3225550848 | bytes 1581056 | tf_op jit(solution)/shard_map/dot_general | solution.py:167
  284.4 6.5 %fusion.26 = f32[2048,64]{0,1:T(8,128)S(1)} fusion(f32[2048,64]{0,1:T(8,128)S(1)} %fusion.27, f32[2048,64]{1,0:T(8,128)S(1)} %bitcast.322, s32[2048]{0:T(1024)S(1)} %get-tuple-element.156), kind=kOutput, calls=%fused_computation.70 | convolution fusion | flops 3225550848 | bytes 1581056 | tf_op jit(solution)/shard_map/dot_general | solution.py:167
  291.7 36.2 %reshape_reshape.7 = f32[8,8,2,8,2,32,2]{4,3,2,1,0,6,5:T(8,128)} reshape(f32[2048,64]{0,1:T(8,128)S(1)} %fusion.26) | data formatting | bytes 1048576 | tf_op jit(solution)/shard_map/reshape;reshape | solution.py:174
  327.9 12.3 %reduce_sum.42 = f32[8,8,8,32]{2,1,0,3:T(8,128)S(1)} reduce(f32[8,8,2,8,2,32,2]{4,3,2,1,0,6,5:T(8,128)} %reshape_reshape.7, f32[]{:T(128)} %constant.240.clone.1), dimensions={2,4,6}, to_apply=%region_6.7 | reduce | flops 114688 | bytes 589828 | tf_op jit(solution)/shard_map/reduce_sum | solution.py:174
  341.9 1.8 all_to_all.20
  343.7 4.7 %all-to-all-start.2 = ((f32[128,1,2048]{2,1,0:T(1,128)}), f32[128,1,2048]{2,1,0:T(1,128)}, u32[]{:S(2)}, u32[]{:S(2)}) async-start(f32[128,1,2048]{2,1,0:T(1,128)} %all_to_all.20), calls=%async_computation.2 | async-start | bytes 2097152 | tf_op jit(solution)/shard_map/all_to_all | solution.py:177
  348.4 3.9 pad_add_fusion
  354.2 1.8 fusion.39
  360.4 1.8 collective-permute-done.1
  362.4 5.0 %reshape.795 = f32[1,8,8,8,32,32]{5,4,3,2,1,0:T(8,128)} reshape(f32[8,64,1024]{2,1,0:T(8,128)S(1)} %scatter-add.18) | data formatting | bytes 4194304 | tf_op jit(solution)/shard_map/reshape | solution.py:182
  367.4 11.3 %copy.150 = f32[1,8,8,8,32,32]{5,3,1,4,2,0:T(8,128)} copy(f32[1,8,8,8,32,32]{5,4,3,2,1,0:T(8,128)} %reshape.795) | data formatting | bytes 4194304 | tf_op jit(solution)/shard_map/reshape | solution.py:182
  378.8 6.4 %reshape.796 = f32[256,2048]{1,0:T(8,128)S(1)} reshape(f32[1,8,32,8,8,32]{5,4,3,2,1,0:T(8,128)} %bitcast.314) | data formatting | bytes 4194304 | tf_op jit(solution)/shard_map/reshape | solution.py:184
  387.8 4.0 scatter_custom_fusion.1
  391.7 5.1 %reshape.805 = f32[1,8,32,8,8,32]{5,4,3,2,1,0:T(8,128)} reshape(f32[256,2048]{1,0:T(8,128)S(1)} %scatter_custom_fusion.1) | data formatting | bytes 4194304 | tf_op jit(solution)/shard_map/reshape | solution.py:188
  396.8 11.4 %copy.119 = f32[1,8,8,8,32,32]{5,4,3,2,1,0:T(8,128)} copy(f32[1,8,8,8,32,32]{5,3,1,4,2,0:T(8,128)} %bitcast.315) | data formatting | bytes 4194304 | tf_op jit(solution)/shard_map/transpose | solution.py:189
  408.3 7.7 %reshape.806 = f32[8,64,1024]{2,1,0:T(8,128)} reshape(f32[1,8,8,8,32,32]{5,4,3,2,1,0:T(8,128)} %copy.119) | data formatting | bytes 4194304 | tf_op jit(solution)/shard_map/reshape | solution.py:190
  (209 shorter events, 68.0 us)
Async XLA Ops:
  0.6 21.5 %copy-start.3 = (f32[3,256,128]{2,1,0:T(8,128)S(1)}, f32[3,256,128]{2,1,0:T(8,128)}, u32[]{:S(2)}) copy-start(f32[3,256,128]{2,1,0:T(8,128)} %param.19) | copy-start | bytes 1179652
  0.6 21.5 %copy-start.6 = (f32[256,128]{1,0:T(8,128)S(1)}, f32[256,128]{1,0:T(8,128)}, u32[]{:S(2)}) copy-start(f32[256,128]{1,0:T(8,128)} %param.20) | copy-start | bytes 393220
  3.1 19.8 %copy-start.8 = (s32[256,128]{1,0:T(8,128)S(1)}, s32[256,128]{1,0:T(8,128)}, u32[]{:S(2)}) copy-start(s32[256,128]{1,0:T(8,128)} %param.18) | copy-start | bytes 393220
  6.3 201.2 %all-to-all-start = ((f32[128,1,16]{2,1,0:T(1,128)}), f32[128,1,16]{2,1,0:T(1,128)}, u32[]{:S(2)}, u32[]{:S(2)}) async-start(f32[128,1,16]{2,1,0:T(1,128)} %bitcast.45), calls=%async_computation | async-start | bytes 131072 | tf_op jit(solution)/shard_map/all_to_all | solution.py:153
  98.0 1.9 copy-start.4
  194.3 3.5 copy-start.5
  207.5 10.2 %copy-start.9 = (s32[256]{0:T(256)S(1)}, s32[256]{0:T(256)}, u32[]{:S(2)}) copy-start(s32[256]{0:T(256)} %param.17) | copy-start | bytes 3076
  207.5 41.1 %all-to-all-start.1 = ((f32[128,16,256]{2,1,0:T(8,128)}), f32[128,16,256]{2,1,0:T(8,128)}, u32[]{:S(2)}, u32[]{:S(2)}) async-start(f32[128,16,256]{2,1,0:T(8,128)} %fusion.22), calls=%async_computation.1 | async-start | bytes 4194304 | tf_op jit(solution)/shard_map/all_to_all | solution.py:152
  225.2 1.5 copy-start
  225.2 2.1 copy-start.1
  225.3 2.8 copy-start.2
  225.3 4.4 %copy-start.11 = (s32[1024]{0:T(1024)S(1)}, s32[1024]{0:T(1024)}, u32[]{:S(2)}) copy-start(s32[1024]{0:T(1024)} %param.26) | copy-start | bytes 12292
  228.0 126.1 %collective-permute-start = (f32[65,1024]{1,0:T(8,128)}, f32[65,1024]{1,0:T(8,128)}, u32[]{:S(2)}, u32[]{:S(2)}) collective-permute-start(f32[65,1024]{1,0:T(8,128)} %add_bitcast_fusion), channel_id=1, source_target_pairs={{0,4},{4,8},{8,12},{12,16},{16,20},{20,24},{24,28},{28,32},{32,36}... | collective-permute-start | bytes 798728 | tf_op jit(solution)/shard_map/ppermute | solution.py:24
  290.9 0.8 copy-start.7
  343.7 44.1 %all-to-all-start.2 = ((f32[128,1,2048]{2,1,0:T(1,128)}), f32[128,1,2048]{2,1,0:T(1,128)}, u32[]{:S(2)}, u32[]{:S(2)}) async-start(f32[128,1,2048]{2,1,0:T(1,128)} %all_to_all.20), calls=%async_computation.2 | async-start | bytes 2097152 | tf_op jit(solution)/shard_map/all_to_all | solution.py:177
  352.2 1.7 copy-start.10
  357.0 5.2 %collective-permute-start.1 = (f32[8,1024]{1,0:T(8,128)S(1)}, f32[8,1024]{1,0:T(8,128)S(1)}, u32[]{:S(2)}, u32[]{:S(2)}) collective-permute-start(f32[8,1024]{1,0:T(8,128)S(1)} %bitcast.329), channel_id=1, source_target_pairs={{0,1},{1,2},{2,3},{3,0},{4,5},{5,6},{6,7},{7,4},{8,9},{9,10},{10,1... | collective-permute-start | bytes 98312 | tf_op jit(solution)/shard_map/ppermute | solution.py:24
where the time goes:
time: 425 us; the launch traced here: 416 us
  local copies, waits for them, and re-layouts  178 us (42%)
  matrix products  101 us (24%)
  other arithmetic  86.5 us (20%)
  starting transfers between devices  30.7 us (7%)
  waiting for transfers between devices  17.9 us (4%)
    dot_general x8, matrix products, block_profiles(): jnp.einsum('tmp,tpl->tml', mixed, lower_hot, precision=highest_precision)  59.4 us
    another operation x1, local copies, waits for them, and re-layouts, shards(): fine_rows.reshape(BPH, BX, 2, BY, 2, BZ, 2).sum(axis=(2, 4, 6))  36.2 us
    dynamic_update_slice x7, local copies, waits for them, and re-layouts, tile_profiles(): result = lax.map(tile_one_group, (zbins_g, fractions_g, masses_g))  31.1 us
    dot_general x4, matrix products, shards(): jnp.dot(target_hot.T, arrived_rows[:, 2 * first + second], precision=high...  26.2 us
    mul x1, other arithmetic, block_profiles(): weights[:, :, None, :] * jnp.swapaxes(upper_hot, 1, 2)[:, None, :, :]  21.5 us
    reshape x2, local copies, waits for them, and re-layouts, shards(): core.reshape(CX // BX, BX, CY // BY, BY, NZ // BZ, BZ)  16.4 us
    all_to_all x1, waiting for transfers between devices, shards(): lax.all_to_all(outgoing, ('blk', 'cross'), split_axis=0, concat_axis=0, t...  16 us
    all_to_all x1, starting transfers between devices, shards(): lax.all_to_all(header, ('blk', 'cross'), split_axis=0, concat_axis=0, til...  12.7 us
  transfers between devices with their start and end apart: 5, of which 2 were waited for; matrix products, arithmetic and copies ran while one was open for 78% of the time, Pallas kernels for 0%

commit v1 on v0

v1 whole, which is shorter than its diff:
```python
import jax
import jax.numpy as jnp
from jax import lax
from jax.experimental import pallas as pl
from jax.experimental.pallas import tpu as pltpu
from jax.sharding import PartitionSpec as P

CX = 8
CY = 64
NZ = 1024
BPH = 8
NODES = 128
PT = 128
BT = 256
FT = 896
GROUPS = FT // 4
SLOTS = 4
GX = CX + 1
GY = CY + 1
AXES = ("blk", "cross")
PARTS = 4
LINE = SLOTS * 1024 + 128
VMEM_BYTES = 62 * 1024 * 1024
f32 = jnp.float32
bf16 = jnp.bfloat16
i32 = jnp.int32


def shifted(value, axis, steps):
    count = lax.axis_size(axis)
    pairs = [(source, (source + steps) % count) for source in range(count)]
    return lax.ppermute(value, axis, pairs)


def diagonal(value):
    blocks, columns = lax.axis_size("blk"), lax.axis_size("cross")
    pairs = [
        (b * columns + c, (b + 1) % blocks * columns + (c + 1) % columns)
        for b in range(blocks)
        for c in range(columns)
    ]
    return lax.ppermute(value, AXES, pairs)


def iota(shape, dim):
    return lax.broadcasted_iota(i32, shape, dim)


def two_terms(value):
    high = value.astype(bf16).astype(f32)
    return high, value - high


def nt_dot(left, right):
    return lax.dot_general(left, right, (((1,), (1,)), ((), ())), preferred_element_type=f32)


def corner_weights(u, v, w, m):
    result = []
    for part_x in (1.0 - u, u):
        row = []
        for part_y in (1.0 - v, v):
            plane = m * part_x * part_y
            row.append((plane * (1.0 - w), plane * w))
        result.append(row)
    return result


def fine_profile_kernel(
    box_ref, boxes_ref, columns_ref, zbin_ref, frac_ref, mass_ref, out_ref, label_ref, head_ref, last_ref
):
    part = pl.program_id(0)

    @pl.when(part == 0)
    def _():
        out_ref[...] = jnp.zeros(out_ref.shape, f32)
        boxes = boxes_ref[...]
        columns = columns_ref[...]
        x = (columns * 4370) >> 16
        y = columns - x * 15
        label_ref[...] = ((y & 1) * 1024 + (x * 8 + (y >> 1)) * 8 + (boxes & 7)).astype(f32)
        head_ref[...] = jnp.zeros((1, 128), f32)
        last_ref[0] = -1

    four_lanes = iota((1, 128), 1) // 4
    sub = iota((8, PT), 0)
    four = sub % 4
    turn = (iota((8, PT), 1) // 32 - four) & 3
    z_row = iota((32, PT), 0).astype(f32).astype(bf16)
    one = jnp.ones((32, PT), bf16)
    zero = jnp.zeros((32, PT), bf16)
    none = jnp.zeros((16, PT), bf16)

    def step(i, carry):
        last, head = carry
        rows = pl.ds(pl.multiple_of(i * 8, 8), 8)
        z = zbin_ref[rows, :]
        weights = corner_weights(frac_ref[0, rows, :], frac_ref[1, rows, :], frac_ref[2, rows, :], mass_ref[rows, :])
        left = []
        right = []
        for e in (0, 1):
            cell = z + e
            upper = (cell >> 5).astype(f32)
            below = jnp.concatenate([upper, upper], axis=0).astype(bf16) == none
            parts = []
            for a in (0, 1):
                for b in (0, 1):
                    terms = jnp.concatenate(two_terms(weights[a][b][e]), axis=0).astype(bf16)
                    parts.append(jnp.where(below, terms, none))
                    parts.append(jnp.where(below, none, terms))
            left.append(jnp.concatenate(parts, axis=0))
            lower = (cell & 31).astype(f32)
            hots = []
            for t in range(8):
                row = jnp.broadcast_to(lower[t:t + 1, :], (32, PT)).astype(bf16)
                hots.append(jnp.where(row == z_row, one, zero))
            right.append(jnp.concatenate(hots, axis=0))
        product = nt_dot(jnp.concatenate(left, axis=1), jnp.concatenate(right, axis=1))
        halves = []
        for a in (0, 1):
            quarters = []
            for q in range(4):
                start = (4 * a + q) * 16
                total = product[start:start + 8, :] + product[start + 8:start + 16, :]
                quarters.append(jnp.where(sub < 4, total[:, 0:128], total[:, 128:256]))
            gathered = None
            for s in range(4):
                value = quarters[s]
                for k in (1, 2, 3):
                    value = jnp.where(four == k, quarters[(k + s) % 4], value)
                if s:
                    value = pltpu.roll(value, 32 * s, 1)
                gathered = value if gathered is None else jnp.where(turn == s, value, gathered)
            halves.append(gathered)
        first = jnp.where(sub < 4, halves[0], pltpu.roll(halves[1], 4, 0))
        second = jnp.where(sub < 4, pltpu.roll(halves[0], 4, 0), halves[1])
        for g, value in ((0, first), (1, second)):
            group = part * (FT // PARTS // 4) + i * 2 + g
            owner = box_ref[group * 4] >> 3
            out_ref[owner, :, pl.ds(pl.multiple_of((group & 3) * 1024, 1024), 1024)] = value.reshape(1, 1024)
            label = jnp.where(four_lanes == (group & 31), label_ref[pl.ds(group >> 5, 1), :], 0.0)
            head = jnp.where(owner == last, head, 0.0) + label
            last = owner
            out_ref[owner, :, 4096:4224] = head
        return last, head

    steps = FT // PARTS // 8
    last, head = lax.fori_loop(0, steps, step, (last_ref[0], head_ref[...]), unroll=steps)
    last_ref[0] = last
    head_ref[...] = head


def fine_profiles(tile_box, fine_column, fine_zbin, fine_frac, fine_weight):
    tiles = FT // PARTS
    return pl.pallas_call(
        fine_profile_kernel,
        out_shape=jax.ShapeDtypeStruct((NODES, 1, LINE), f32),
        grid=(PARTS,),
        in_specs=[
            pl.BlockSpec(memory_space=pltpu.SMEM),
            pl.BlockSpec((FT // 128, 128), lambda i: (0, 0)),
            pl.BlockSpec((FT // 128, 128), lambda i: (0, 0)),
            pl.BlockSpec((tiles, PT), lambda i: (i, 0)),
            pl.BlockSpec((3, tiles, PT), lambda i: (0, i, 0)),
            pl.BlockSpec((tiles, PT), lambda i: (i, 0)),
        ],
        out_specs=pl.BlockSpec((NODES, 1, LINE), lambda i: (0, 0, 0)),
        scratch_shapes=[
            pltpu.VMEM((FT // 128, 128), f32),
            pltpu.VMEM((1, 128), f32),
            pltpu.SMEM((1,), i32),
        ],
        compiler_params=pltpu.CompilerParams(vmem_limit_bytes=VMEM_BYTES),
        cost_estimate=pl.CostEstimate(flops=2 * 128 * 256 * 256 * 112, bytes_accessed=4500000, transcendentals=0),
        name="fine_profiles",
    )(
        tile_box,
        tile_box.reshape(FT // 128, 128),
        fine_column.reshape(FT // 128, 128),
        fine_zbin,
        fine_frac,
        fine_weight,
    )


def tables_kernel(me_ref, home_ref, anchor_ref, owner_ref, place_ref):
    index = iota((8, 128), 0) * 128 + iota((8, 128), 1)
    left = jnp.where(home_ref[...] == me_ref[0], index, NODES * BPH)
    for n in range(BPH):
        box = jnp.minimum(jnp.min(left), NODES * BPH - 1)
        left = jnp.where(left == box, NODES * BPH, left)
        owner_ref[n] = box >> 3
        place_ref[n] = anchor_ref[box]


def tables(me, box_home, box_anchor):
    smem = pl.BlockSpec(memory_space=pltpu.SMEM)
    return pl.pallas_call(
        tables_kernel,
        out_shape=(jax.ShapeDtypeStruct((BPH,), i32), jax.ShapeDtypeStruct((BPH,), i32)),
        in_specs=[smem, pl.BlockSpec(memory_space=pltpu.VMEM), smem],
        out_specs=(smem, smem),
        cost_estimate=pl.CostEstimate(flops=4000000, bytes_accessed=40000, transcendentals=0),
        name="tables",
    )(me, box_home.reshape(8, 128), box_anchor)


def base_kernel(column_ref, zbin_ref, frac_ref, mass_ref, core_ref, front_ref, side_ref, corner_ref, grid_ref):
    grid_ref[...] = jnp.zeros(grid_ref.shape, f32)
    upper_row = iota((8, PT), 0)
    lower_row = iota((128, PT), 0)

    def step(i, carry):
        rows = pl.ds(pl.multiple_of(i * 8, 8), 8)
        z = zbin_ref[rows, :]
        weights = corner_weights(frac_ref[0, rows, :], frac_ref[1, rows, :], frac_ref[2, rows, :], mass_ref[rows, :])
        cells = (z, (z + 1) & (NZ - 1))
        uppers = [cell >> 7 for cell in cells]
        lowers = [cell & 127 for cell in cells]
        for t in range(8):
            left = []
            right = []
            for e in (0, 1):
                mask = jnp.broadcast_to(uppers[e][t:t + 1, :], (8, PT)) == upper_row
                parts = []
                for a in (0, 1):
                    for b in (0, 1):
                        row = jnp.broadcast_to(weights[a][b][e][t:t + 1, :], (8, PT))
                        parts.extend(two_terms(jnp.where(mask, row, 0.0)))
                left.append(jnp.concatenate(parts, axis=0).astype(bf16))
                low = jnp.broadcast_to(lowers[e][t:t + 1, :], (128, PT))
                right.append(jnp.where(low == lower_row, 1.0, 0.0).astype(bf16))
            product = nt_dot(jnp.concatenate(left, axis=1), jnp.concatenate(right, axis=1))
            q = column_ref[i * 8 + t]
            corner = (q // CY) * GY + q % CY
            for a in (0, 1):
                for b in (0, 1):
                    start = (2 * a + b) * 16
                    place = pl.ds(pl.multiple_of((corner + a * GY + b) * 8, 8), 8)
                    grid_ref[place, :] += product[start:start + 8, :] + product[start + 8:start + 16, :]
        return carry

    lax.fori_loop(0, BT // 8, step, 0)
    for x in range(GX):
        for band in range(CY // 8):
            for part in range(8):
                rows = grid_ref[pl.ds((x * GY + band * 8) * 8 + part, 8, stride=8), :]
                if x < CX:
                    core_ref[x, band * 8:band * 8 + 8, part * 128:part * 128 + 128] = rows
                else:
                    front_ref[band * 8:band * 8 + 8, part * 128:part * 128 + 128] = rows
    for part in range(8):
        lanes = slice(part * 128, part * 128 + 128)
        side_ref[:, lanes] = grid_ref[pl.ds(CY * 8 + part, 8, stride=GY * 8), :]
        corner_row = (CX * GY + CY) * 8 + part
        corner_ref[0:1, lanes] = grid_ref[corner_row:corner_row + 1, :]


def base_deposit(base_column, base_zbin, base_frac, base_weight):
    vmem = pl.BlockSpec(memory_space=pltpu.VMEM)
    return pl.pallas_call(
        base_kernel,
        out_shape=(
            jax.ShapeDtypeStruct((CX, CY, NZ), f32),
            jax.ShapeDtypeStruct((CY, NZ), f32),
            jax.ShapeDtypeStruct((CX, NZ), f32),
            jax.ShapeDtypeStruct((1, NZ), f32),
        ),
        in_specs=[pl.BlockSpec(memory_space=pltpu.SMEM), vmem, vmem, vmem],
        out_specs=(vmem, vmem, vmem, vmem),
        scratch_shapes=[pltpu.VMEM((GX * GY * 8, 128), f32)],
        compiler_params=pltpu.CompilerParams(vmem_limit_bytes=VMEM_BYTES),
        cost_estimate=pl.CostEstimate(flops=10000000000, bytes_accessed=5000000, transcendentals=0),
        name="base_deposit",
    )(base_column, base_zbin, base_frac, base_weight)


def halo_kernel(core_ref, front_ref, side_ref, corner_ref, out_ref):
    out_ref[...] = core_ref[...]
    out_ref[0, :, :] += front_ref[...]
    out_ref[:, 0, :] += side_ref[...]
    out_ref[0, 0:1, :] += corner_ref[...]


def halo_add(core, front, side, corner):
    vmem = pl.BlockSpec(memory_space=pltpu.VMEM)
    return pl.pallas_call(
        halo_kernel,
        out_shape=jax.ShapeDtypeStruct((CX, CY, NZ), f32),
        in_specs=[vmem] * 4,
        out_specs=vmem,
        compiler_params=pltpu.CompilerParams(vmem_limit_bytes=VMEM_BYTES),
        cost_estimate=pl.CostEstimate(flops=1000000, bytes_accessed=4500000, transcendentals=0),
        name="halo_add",
    )(core, front, side, corner)


ROWS = NODES * SLOTS * 8
MB = 256
KB = 512


def arrival_rows(heads):
    line = iota((128, 128), 0)
    lane = iota((128, 128), 1)
    spread = jnp.where(line % 16 == (lane // 8) % 4 * 4 + lane % 4, 1.0, 0.0).astype(bf16)
    labels = (heads + 0.5).astype(i32)
    digits = jnp.concatenate([(labels >> 4).astype(f32), (labels & 15).astype(f32)], axis=0).astype(bf16)
    wide = jnp.dot(digits, spread, preferred_element_type=f32)
    wide = wide[0:16, :] * 16.0 + wide[16:32, :]
    wide = jnp.where(iota((16, 128), 0) % 4 == iota((16, 128), 1) // 32, wide, 0.0)
    shift = 64 * ((iota((1, 128), 1) // 4) % 2)
    return [
        (jnp.sum(wide[4 * k:4 * k + 4, :], axis=0, keepdims=True) + 0.5).astype(i32) + shift for k in range(4)
    ]


def arrival_terms(got_ref):
    count = got_ref.shape[0]
    parts = [got_ref[s, :, 0:SLOTS * 1024].reshape(SLOTS * 8, 128) for s in range(count)]
    high, low = two_terms(jnp.concatenate(parts, axis=0))
    return high.astype(bf16), low.astype(bf16)


def coarse_kernel(home_ref, got_ref, send_ref, head_ref, sums_ref, part_ref, sem):
    step = pl.program_id(0)
    terms = jnp.concatenate(arrival_terms(got_ref), axis=1)
    lines = []
    for k, row in enumerate(arrival_rows(got_ref[:, 0, SLOTS * 1024:LINE])):
        head_ref[pl.ds(step * (KB // 128) + k, 1), :] = row
        lines.append((row >> 10) * 512 + ((row >> 7) & 7) * 64 + (row & 63))

    @pl.when(step == 0)
    def _():
        sums_ref[...] = jnp.zeros(sums_ref.shape, f32)

    for m in range(1024 // MB):
        target = iota((MB, 128), 0) + m * MB
        hot = jnp.concatenate(
            [jnp.where(jnp.broadcast_to(line, (MB, 128)) == target, 1.0, 0.0).astype(bf16) for line in lines], axis=1
        )
        product = jnp.dot(hot, terms, preferred_element_type=f32)
        sums_ref[m * MB:(m + 1) * MB, :] += product[:, 0:128] + product[:, 128:256]

    @pl.when(step == ROWS // KB - 1)
    def _():
        lane = iota((64, 128), 1)
        fold_row = iota((512, 128), 0)
        fold_lane = iota((512, 128), 1)
        fold = jnp.where((fold_row // 128) * 32 + (fold_row % 64) // 2 == fold_lane, 1.0, 0.0).astype(bf16)
        for far in (0, 1):
            pieces = []
            for q in range(4):
                spot = (4 * far + q) * 64
                odd = sums_ref[512 + spot:512 + spot + 64, :]
                before = jnp.concatenate([jnp.zeros((8, 128), f32), odd[0:56, :]], axis=0)
                both = sums_ref[spot:spot + 64, :] + jnp.where(lane < 64, odd, before)
                pieces.append(jnp.concatenate(two_terms(both), axis=0).astype(bf16))
            folded = jnp.dot(jnp.concatenate(pieces, axis=1), fold, preferred_element_type=f32)
            part_ref[far * 64:far * 64 + 64, :] = folded[0:64, :] + folded[64:128, :]
        copies = []
        for box in range(BPH):
            for far in (0, 1):
                hot = part_ref[pl.ds(far * 64 + box, 8, stride=8), :]
                part_ref[128 + box * 16 + far * 8:128 + box * 16 + far * 8 + 8, :] = hot
        for box in range(BPH):
            copy = pltpu.make_async_copy(
                part_ref.at[pl.ds(128 + box * 16, 16), :], send_ref.at[home_ref[box]], sem.at[box]
            )
            copy.start()
            copies.append(copy)
        for copy in copies:
            copy.wait()


def coarse_deposit(homes, arrived):
    return pl.pallas_call(
        coarse_kernel,
        out_shape=(jax.ShapeDtypeStruct((NODES, 16, 128), f32), jax.ShapeDtypeStruct((32, 128), i32)),
        grid=(ROWS // KB,),
        in_specs=[
            pl.BlockSpec(memory_space=pltpu.SMEM),
            pl.BlockSpec((16, 1, LINE), lambda i: (i, 0, 0)),
        ],
        out_specs=(pl.BlockSpec(memory_space=pl.ANY), pl.BlockSpec((32, 128), lambda i: (0, 0))),
        scratch_shapes=[
            pltpu.VMEM((1024, 128), f32),
            pltpu.VMEM((256, 128), f32),
            pltpu.SemaphoreType.DMA((BPH,)),
        ],
        compiler_params=pltpu.CompilerParams(vmem_limit_bytes=VMEM_BYTES),
        cost_estimate=pl.CostEstimate(flops=2 * 1024 * ROWS * 256, bytes_accessed=2200000, transcendentals=0),
        name="coarse_deposit",
    )(homes, arrived)


def fine_kernel(head_ref, got_ref, fine_ref, terms_ref, sums_ref, hot_ref):
    high, low = arrival_terms(got_ref)
    terms_ref[:, 0:128] = high
    terms_ref[:, 128:256] = low

    def block(m, carry):
        target = iota((MB, 128), 0) + m * MB
        for k in range(ROWS // 128):
            row = jnp.broadcast_to(head_ref[k:k + 1, :], (MB, 128))
            hot_ref[:, k * 128:k * 128 + 128] = jnp.where(row == target, 1.0, 0.0).astype(bf16)
        product = jnp.dot(hot_ref[...], terms_ref[...], preferred_element_type=f32)
        sums_ref[pl.ds(pl.multiple_of(m * MB, MB), MB), :] = product[:, 0:128] + product[:, 128:256]
        return carry

    lax.fori_loop(0, 2048 // MB, block, 0)
    lane = iota((8, 128), 1)
    for x in range(16):
        for y in range(8):
            spot = (x * 8 + y) * 8
            odd = sums_ref[1024 + spot:1024 + spot + 8, :]
            before = sums_ref[1024 + spot - 8:1024 + spot, :] if y else jnp.zeros((8, 128), f32)
            cross = pltpu.roll(jnp.where(lane < 64, odd, before), 64, 1)
            fine_ref[:, spot * 16:spot * 16 + 128] = sums_ref[spot:spot + 8, :] + cross


def fine_deposit(header, arrived):
    vmem = pl.BlockSpec(memory_space=pltpu.VMEM)
    return pl.pallas_call(
        fine_kernel,
        out_shape=jax.ShapeDtypeStruct((BPH, 16384), f32),
        in_specs=[vmem, vmem],
        out_specs=vmem,
        scratch_shapes=[
            pltpu.VMEM((ROWS, 256), bf16),
            pltpu.VMEM((2048, 128), f32),
            pltpu.VMEM((MB, ROWS), bf16),
        ],
        compiler_params=pltpu.CompilerParams(vmem_limit_bytes=VMEM_BYTES),
        cost_estimate=pl.CostEstimate(flops=2 * 2048 * ROWS * 256, bytes_accessed=4000000, transcendentals=0),
        name="fine_deposit",
    )(header, arrived)


def lattice_kernel(owner_ref, place_ref, base_ref, got_ref, out_ref, held_ref, block_ref, got_sem, in_sem, out_sem):
    def spot_of(n, grid):
        place = place_ref[n]
        rows = pl.ds(pl.multiple_of(((place >> 5) & 7) * 8, 8), 8)
        lanes = pl.ds(pl.multiple_of(((place >> 2) & 7) * 128, 128), 128)
        return grid.at[:, rows, lanes]

    copies = []
    for n in range(BPH):
        copies.append(pltpu.make_async_copy(got_ref.at[owner_ref[n]], held_ref.at[n], got_sem.at[n]))
        copies.append(pltpu.make_async_copy(spot_of(n, base_ref), block_ref.at[n], in_sem.at[n]))
    for copy in copies:
        copy.start()
    firsts = []
    for n in range(BPH):
        first = jnp.int32(n)
        for k in reversed(range(n)):
            first = jnp.where(place_ref[k] >> 2 == place_ref[n] >> 2, k, first)
        firsts.append(first)
    for copy in copies:
        copy.wait()
    quarter = iota((8, 128), 1) // 32
    for n in range(BPH):
        spot = place_ref[n] & 3
        for x in range(CX):
            value = held_ref[n, (x // 4) * 8:(x // 4) * 8 + 8, :]
            moved = pltpu.roll(value, ((spot - x % 4 + 4) & 3) * 32, 1)
            block_ref[firsts[n], x] += jnp.where(quarter == spot, moved, 0.0)
    for n in range(BPH):
        @pl.when(firsts[n] == n)
        def _():
            pltpu.make_async_copy(block_ref.at[n], spot_of(n, out_ref), out_sem.at[n]).start()
    for n in range(BPH):
        @pl.when(firsts[n] == n)
        def _():
            pltpu.make_async_copy(block_ref.at[n], spot_of(n, out_ref), out_sem.at[n]).wait()


def lattice_add(owners, places, base, arrived):
    smem = pl.BlockSpec(memory_space=pltpu.SMEM)
    hbm = pl.BlockSpec(memory_space=pl.ANY)
    return pl.pallas_call(
        lattice_kernel,
        out_shape=jax.ShapeDtypeStruct((CX, CY, NZ), f32),
        in_specs=[smem, smem, hbm, hbm],
        out_specs=hbm,
        input_output_aliases={2: 0},
        scratch_shapes=[
            pltpu.VMEM((BPH, 16, 128), f32),
            pltpu.VMEM((BPH, CX, 8, 128), f32),
            pltpu.SemaphoreType.DMA((BPH,)),
            pltpu.SemaphoreType.DMA((BPH,)),
            pltpu.SemaphoreType.DMA((BPH,)),
        ],
        compiler_params=pltpu.CompilerParams(vmem_limit_bytes=VMEM_BYTES),
        cost_estimate=pl.CostEstimate(flops=1000000, bytes_accessed=1000000, transcendentals=0),
        name="lattice_add",
    )(owners, places, base, arrived)


def shards(
    base_column,
    base_zbin,
    base_frac,
    base_weight,
    fine_column,
    fine_zbin,
    fine_frac,
    fine_weight,
    tile_box,
    box_home,
    box_anchor,
):
    myself = lax.axis_index(AXES).astype(i32)
    homes = lax.dynamic_slice_in_dim(box_home, myself * BPH, BPH, 0)
    outgoing = fine_profiles(tile_box, fine_column, fine_zbin, fine_frac, fine_weight)
    outgoing, base_column, myself = lax.optimization_barrier((outgoing, base_column, myself))
    arrived = lax.all_to_all(outgoing, AXES, split_axis=0, concat_axis=0, tiled=True)
    owners, places = tables(myself.reshape(1), box_home, box_anchor)
    core, front, side, corner = base_deposit(base_column, base_zbin, base_frac, base_weight)
    front = shifted(front, "blk", 1)
    side = shifted(side, "cross", 1)
    corner = diagonal(corner)
    arrived, core, front, side, corner, owners, places = lax.optimization_barrier(
        (arrived, core, front, side, corner, owners, places)
    )
    sending, header = coarse_deposit(homes, arrived)
    sending, header, core = lax.optimization_barrier((sending, header, core))
    returned = lax.all_to_all(sending, AXES, split_axis=0, concat_axis=0, tiled=True)
    fine_rows = fine_deposit(header, arrived)
    base = halo_add(core, front, side, corner)
    returned, base, fine_rows = lax.optimization_barrier((returned, base, fine_rows))
    base_out = lattice_add(owners, places, base, returned)
    return (base_out, fine_rows)


def solution(mesh):
    placed = (
        P(("blk", "cross")),
        P(("blk", "cross"), None),
        P(None, ("blk", "cross"), None),
        P(("blk", "cross"), None),
        P(("blk", "cross")),
        P(("blk", "cross"), None),
        P(None, ("blk", "cross"), None),
        P(("blk", "cross"), None),
        P(("blk", "cross")),
        P(),
        P(),
    )
    return jax.shard_map(
        shards,
        mesh=mesh,
        in_specs=placed,
        out_specs=(P("blk", "cross", None), P(("blk", "cross"), None)),
        check_vma=False,
    )
```

time: 425 us -> 92 us (0.22); the launches traced: 416 us -> 91.4 us
  local copies, waits for them, and re-layouts: 178 us -> 2.33 us
  matrix products: 101 us -> 0 us
  other arithmetic: 86.5 us -> 0 us
  Pallas kernels: 0 us -> 48.4 us
  starting transfers between devices: 30.7 us -> 22.7 us
    dot_general x15 -> x0, matrix products: 101 us -> none  [the longest x8 59.4 us: block_profiles(): jnp.einsum('tmp,tpl->tml', mixed, lower_hot, precision=highest_precision)]
    pallas_call x0 -> x7, Pallas kernels: none -> 48.4 us  [the longest x1 12.9 us: base_deposit(): pl.pallas_call(base_kernel, out_shape=(jax.ShapeDtypeStruct((CX, CY, NZ),...]
    reshape x9 -> x0, local copies, waits for them, and re-layouts: 42 us -> none  [the longest x2 16.4 us: shards(): core.reshape(CX // BX, BX, CY // BY, BY, NZ // BZ, BZ)]
    another operation x11 -> x0, local copies, waits for them, and re-layouts: 40.5 us -> none  [the longest x1 36.2 us: shards(): fine_rows.reshape(BPH, BX, 2, BY, 2, BZ, 2).sum(axis=(2, 4, 6))]
    dynamic_update_slice x7 -> x0, local copies, waits for them, and re-layouts: 31.1 us -> none  [tile_profiles(): result = lax.map(tile_one_group, (zbins_g, fractions_g, masses_g))]
    mul x1 -> x0, other arithmetic: 21.5 us -> none  [block_profiles(): weights[:, :, None, :] * jnp.swapaxes(upper_hot, 1, 2)[:, None, :, :]]
    slice x6 -> x0, local copies, waits for them, and re-layouts: 21.4 us -> none  [the longest x1 11 us: shards(): arrived_rows[:, 2 * first + second]]
    select_n x18 -> x0, other arithmetic: 13.3 us -> none  [the longest x8 6.27 us: block_profiles(): zbins[:, :, None] % lower == jnp.arange(lower, dtype=jnp.int32)]
  transfers between devices with their start and end apart: 5 -> 5, of which waited for: 2 -> 3; matrix products, arithmetic and copies ran while one was open for 78% -> 1% of each run, Pallas kernels for 0% -> 31%
where the time goes in v1:
time: 92 us; the launch traced here: 91.4 us
  Pallas kernels  48.4 us (53%)
  starting transfers between devices  22.7 us (25%)
  waiting for transfers between devices  17.2 us (19%)
  local copies, waits for them, and re-layouts  2.33 us (3%)
    pallas_call x1, Pallas kernels, base_deposit(): pl.pallas_call(base_kernel, out_shape=(jax.ShapeDtypeStruct((CX, CY, NZ),...  12.9 us
    all_to_all x1, starting transfers between devices, shards(): lax.all_to_all(outgoing, AXES, split_axis=0, concat_axis=0, tiled=True)  11.9 us
    pallas_call x1, Pallas kernels, fine_deposit(): pl.pallas_call(fine_kernel, out_shape=jax.ShapeDtypeStruct((BPH, 16384),...  9.12 us
    pallas_call x1, Pallas kernels, coarse_deposit(): pl.pallas_call(coarse_kernel, out_shape=(jax.ShapeDtypeStruct((NODES, 16,...  8.96 us
    pallas_call x1, Pallas kernels, fine_profiles(): pl.pallas_call(fine_profile_kernel, out_shape=jax.ShapeDtypeStruct((NODES...  8.53 us
    all_to_all x1, waiting for transfers between devices, shards(): lax.all_to_all(sending, AXES, split_axis=0, concat_axis=0, tiled=True)  7.43 us
    all_to_all x1, starting transfers between devices, shards(): lax.all_to_all(sending, AXES, split_axis=0, concat_axis=0, tiled=True)  6.23 us
    all_to_all x1, waiting for transfers between devices, shards(): lax.all_to_all(outgoing, AXES, split_axis=0, concat_axis=0, tiled=True)  6.08 us
  transfers between devices with their start and end apart: 5, of which 3 were waited for; matrix products, arithmetic and copies ran while one was open for 1% of the time, Pallas kernels for 31%

profile of v1, /device:TPU:1, one launch (start us, length us, event | category | flops | bytes accessed | tf_op | source)
XLA Modules:
  0.0 91.4 jit_solution(9860480791568476684)
XLA Ops:
  0.6 8.5 %fine_profiles.1 = f32[128,1,4224]{2,1,0:T(1,128)} custom-call(s32[896]{0:T(1024)} %box_ref.1, s32[7,128]{1,0:T(8,128)} %bitcast.4, s32[7,128]{1,0:T(8,128)} %bitcast.5, s32[896,128]{1,0:T(8,128)} %zbin_ref.2, f32[3,896,128]{2,1,0:T(8,128)} %frac_ref.2, f32[896,128]{1,0:T(8,128)} %mass_ref.2), custom_call_target="tpu_custom_call" | custom-call | flops 1879048192 | bytes 4500000 | tf_op jit(solution)/shard_map/fine_profiles/pallas_call | solution.py:155
  9.2 11.9 %all-to-all-start = ((f32[128,1,4224]{2,1,0:T(1,128)}), f32[128,1,4224]{2,1,0:T(1,128)}, u32[]{:S(2)}, u32[]{:S(2)}) async-start(f32[128,1,4224]{2,1,0:T(1,128)} %fine_profiles.1), calls=%async_computation | async-start | bytes 4325376 | tf_op jit(solution)/shard_map/all_to_all | solution.py:517
  21.1 12.9 %base_deposit.1 = (f32[8,64,1024]{2,1,0:T(8,128)}, f32[64,1024]{1,0:T(8,128)}, f32[8,1024]{1,0:T(8,128)}, f32[1,1024]{1,0:T(1,128)}) custom-call(s32[256]{0:T(256)} %column_ref, s32[256,128]{1,0:T(8,128)} %zbin_ref.3, f32[3,256,128]{2,1,0:T(8,128)} %frac_ref.3, f32[256,128]{1,0:T(8,128)} %mass_ref.3), custom_call_target="tpu_custom_call" | custom-call | flops 10000000000 | bytes 5000000 | tf_op jit(solution)/shard_map/base_deposit/pallas_call | solution.py:261
  34.0 1.6 %collective-permute-start = (f32[64,1024]{1,0:T(8,128)}, f32[64,1024]{1,0:T(8,128)S(1)}, u32[]{:S(2)}, u32[]{:S(2)}) collective-permute-start(f32[64,1024]{1,0:T(8,128)} %get-tuple-element.29), channel_id=1, source_target_pairs={{0,4},{4,8},{8,12},{12,16},{16,20},{20,24},{24,28},{28,32},{32,36}... | collective-permute-start | bytes 786440 | tf_op jit(solution)/shard_map/ppermute | solution.py:32
  35.6 1.4 %collective-permute-start.1 = (f32[8,1024]{1,0:T(8,128)}, f32[8,1024]{1,0:T(8,128)S(1)}, u32[]{:S(2)}, u32[]{:S(2)}) collective-permute-start(f32[8,1024]{1,0:T(8,128)} %get-tuple-element.30), channel_id=1, source_target_pairs={{0,1},{1,2},{2,3},{3,0},{4,5},{5,6},{6,7},{7,4},{8,9},{9,10},{10,1... | collective-permute-start | bytes 98312 | tf_op jit(solution)/shard_map/ppermute | solution.py:32
  37.0 1.6 %collective-permute-start.2 = (f32[1,1024]{1,0:T(1,128)}, f32[1,1024]{1,0:T(1,128)S(1)}, u32[]{:S(2)}, u32[]{:S(2)}) collective-permute-start(f32[1,1024]{1,0:T(1,128)} %get-tuple-element.31), channel_id=1, source_target_pairs={{0,5},{1,6},{2,7},{3,4},{4,9},{5,10},{6,11},{7,8},{8,13},{9,14},{1... | collective-permute-start | bytes 12296 | tf_op jit(solution)/shard_map/ppermute | solution.py:42
  38.6 1.3 %dynamic_slice.3.home_ref = s32[8]{0:T(128)} dynamic-slice(s32[1024]{0:T(1024)} %param.20, s32[]{:T(128)S(6)} %select_n.3), dynamic_slice_sizes={8} | dynamic-slice | bytes 68 | tf_op jit(solution)/shard_map/dynamic_slice | solution.py:514
  40.0 3.0 %tables.1 = (s32[8]{0:T(128)}, s32[8]{0:T(128)}) custom-call(s32[1]{0:T(128)} %bitcast.2.me_ref, s32[8,128]{1,0:T(8,128)} %bitcast.6, s32[1024]{0:T(1024)} %anchor_ref.1), custom_call_target="tpu_custom_call" | custom-call | flops 4000000 | bytes 40000 | tf_op jit(solution)/shard_map/tables/pallas_call | solution.py:198
  42.9 3.7 %collective-permute-done.2.corner_ref = f32[1,1024]{1,0:T(1,128)S(1)} collective-permute-done((f32[1,1024]{1,0:T(1,128)}, f32[1,1024]{1,0:T(1,128)S(1)}, u32[]{:S(2)}, u32[]{:S(2)}) %collective-permute-start.2) | collective-permute-done | bytes 4128 | tf_op jit(solution)/shard_map/ppermute | solution.py:42
  46.6 0.0 copy-start.3
  46.6 0.0 collective-permute-done.1.side_ref
  46.6 0.0 copy-start.2
  46.6 0.0 collective-permute-done.front_ref
  46.7 0.0 copy-start.1
  46.7 6.1 %all-to-all-done.got_ref = f32[128,1,4224]{2,1,0:T(1,128)} async-done(((f32[128,1,4224]{2,1,0:T(1,128)}), f32[128,1,4224]{2,1,0:T(1,128)}, u32[]{:S(2)}, u32[]{:S(2)}) %all-to-all-start) | async-done | bytes 2162720 | tf_op jit(solution)/shard_map/all_to_all | solution.py:517
  52.7 9.0 %coarse_deposit.1 = (f32[128,16,128]{2,1,0:T(8,128)}, s32[32,128]{1,0:T(8,128)}) custom-call(s32[8]{0:T(128)} %dynamic_slice.3.home_ref, f32[128,1,4224]{2,1,0:T(1,128)} %all-to-all-done.got_ref), custom_call_target="tpu_custom_call" | custom-call | flops 2147483648 | bytes 2200000 | tf_op jit(solution)/shard_map/coarse_deposit/pallas_call | solution.py:377
  61.7 0.0 copy-done.3
  61.7 0.0 copy-done.2
  61.7 0.0 copy-done.1
  61.7 6.2 %all-to-all-start.1 = ((f32[128,16,128]{2,1,0:T(8,128)}), f32[128,16,128]{2,1,0:T(8,128)S(1)}, u32[]{:S(2)}, u32[]{:S(2)}) async-start(f32[128,16,128]{2,1,0:T(8,128)} %get-tuple-element.41), calls=%async_computation.1 | async-start | bytes 2097152 | tf_op jit(solution)/shard_map/all_to_all | solution.py:528
  68.0 3.2 %halo_add.1.base_ref = f32[8,64,1024]{2,1,0:T(8,128)} custom-call(f32[8,64,1024]{2,1,0:T(8,128)} %get-tuple-element.42.core_ref, f32[64,1024]{1,0:T(8,128)} %copy-done.1, f32[8,1024]{1,0:T(8,128)} %copy-done.2, f32[1,1024]{1,0:T(1,128)} %copy-done.3), custom_call_target="tpu_custom_call" | custom-call | flops 1000000 | bytes 4500000 | tf_op jit(solution)/shard_map/halo_add/pallas_call | solution.py:287
  71.2 9.1 %fine_deposit.1 = f32[8,16384]{1,0:T(8,128)} custom-call(s32[32,128]{1,0:T(8,128)} %get-tuple-element.46.head_ref, f32[128,1,4224]{2,1,0:T(1,128)} %all-to-all-done.got_ref), custom_call_target="tpu_custom_call" | custom-call | flops 4294967296 | bytes 4000000 | tf_op jit(solution)/shard_map/fine_deposit/pallas_call | solution.py:424
  80.3 7.4 %all-to-all-done.1.got_ref = f32[128,16,128]{2,1,0:T(8,128)S(1)} async-done(((f32[128,16,128]{2,1,0:T(8,128)}), f32[128,16,128]{2,1,0:T(8,128)S(1)}, u32[]{:S(2)}, u32[]{:S(2)}) %all-to-all-start.1) | async-done | bytes 1048608 | tf_op jit(solution)/shard_map/all_to_all | solution.py:528
  87.7 0.0 copy-start
  87.7 1.0 %copy-done = f32[128,16,128]{2,1,0:T(8,128)} copy-done((f32[128,16,128]{2,1,0:T(8,128)}, f32[128,16,128]{2,1,0:T(8,128)S(1)}, u32[]{:S(2)}) %copy-start) | copy-done | bytes 1048600
  88.7 2.7 %lattice_add.1 = f32[8,64,1024]{2,1,0:T(8,128)} custom-call(s32[8]{0:T(128)} %get-tuple-element.35.owner_ref, s32[8]{0:T(128)} %get-tuple-element.36.place_ref, f32[8,64,1024]{2,1,0:T(8,128)} %halo_add.1.base_ref, f32[128,16,128]{2,1,0:T(8,128)} %copy-done), custom_call_target="tpu_custom_call", output_to_operand_aliasing={{}: (2, {})} | custom-call | flops 1000000 | bytes 1000000 | tf_op jit(solution)/shard_map/lattice_add/pallas_call | solution.py:481
Async XLA Ops:
  9.2 43.6 %all-to-all-start = ((f32[128,1,4224]{2,1,0:T(1,128)}), f32[128,1,4224]{2,1,0:T(1,128)}, u32[]{:S(2)}, u32[]{:S(2)}) async-start(f32[128,1,4224]{2,1,0:T(1,128)} %fine_profiles.1), calls=%async_computation | async-start | bytes 4325376 | tf_op jit(solution)/shard_map/all_to_all | solution.py:517
  34.0 12.6 %collective-permute-start = (f32[64,1024]{1,0:T(8,128)}, f32[64,1024]{1,0:T(8,128)S(1)}, u32[]{:S(2)}, u32[]{:S(2)}) collective-permute-start(f32[64,1024]{1,0:T(8,128)} %get-tuple-element.29), channel_id=1, source_target_pairs={{0,4},{4,8},{8,12},{12,16},{16,20},{20,24},{24,28},{28,32},{32,36}... | collective-permute-start | bytes 786440 | tf_op jit(solution)/shard_map/ppermute | solution.py:32
  35.6 11.0 %collective-permute-start.1 = (f32[8,1024]{1,0:T(8,128)}, f32[8,1024]{1,0:T(8,128)S(1)}, u32[]{:S(2)}, u32[]{:S(2)}) collective-permute-start(f32[8,1024]{1,0:T(8,128)} %get-tuple-element.30), channel_id=1, source_target_pairs={{0,1},{1,2},{2,3},{3,0},{4,5},{5,6},{6,7},{7,4},{8,9},{9,10},{10,1... | collective-permute-start | bytes 98312 | tf_op jit(solution)/shard_map/ppermute | solution.py:32
  37.0 9.6 %collective-permute-start.2 = (f32[1,1024]{1,0:T(1,128)}, f32[1,1024]{1,0:T(1,128)S(1)}, u32[]{:S(2)}, u32[]{:S(2)}) collective-permute-start(f32[1,1024]{1,0:T(1,128)} %get-tuple-element.31), channel_id=1, source_target_pairs={{0,5},{1,6},{2,7},{3,4},{4,9},{5,10},{6,11},{7,8},{8,13},{9,14},{1... | collective-permute-start | bytes 12296 | tf_op jit(solution)/shard_map/ppermute | solution.py:42
  46.6 15.1 %copy-start.3 = (f32[1,1024]{1,0:T(1,128)}, f32[1,1024]{1,0:T(1,128)S(1)}, u32[]{:S(2)}) copy-start(f32[1,1024]{1,0:T(1,128)S(1)} %collective-permute-done.2.corner_ref) | copy-start | bytes 12292
  46.6 15.1 %copy-start.2 = (f32[8,1024]{1,0:T(8,128)}, f32[8,1024]{1,0:T(8,128)S(1)}, u32[]{:S(2)}) copy-start(f32[8,1024]{1,0:T(8,128)S(1)} %collective-permute-done.1.side_ref) | copy-start | bytes 98308
  46.7 15.1 %copy-start.1 = (f32[64,1024]{1,0:T(8,128)}, f32[64,1024]{1,0:T(8,128)S(1)}, u32[]{:S(2)}) copy-start(f32[64,1024]{1,0:T(8,128)S(1)} %collective-permute-done.front_ref) | copy-start | bytes 786436
  61.7 26.0 %all-to-all-start.1 = ((f32[128,16,128]{2,1,0:T(8,128)}), f32[128,16,128]{2,1,0:T(8,128)S(1)}, u32[]{:S(2)}, u32[]{:S(2)}) async-start(f32[128,16,128]{2,1,0:T(8,128)} %get-tuple-element.41), calls=%async_computation.1 | async-start | bytes 2097152 | tf_op jit(solution)/shard_map/all_to_all | solution.py:528
  87.7 1.0 %copy-start = (f32[128,16,128]{2,1,0:T(8,128)}, f32[128,16,128]{2,1,0:T(8,128)S(1)}, u32[]{:S(2)}) copy-start(f32[128,16,128]{2,1,0:T(8,128)S(1)} %all-to-all-done.1.got_ref) | copy-start | bytes 3145732

commit v2 on v1

--- a/solution.py
+++ b/solution.py
@@ -21,6 +21,7 @@
 PARTS = 4
 LINE = SLOTS * 1024 + 128
 VMEM_BYTES = 62 * 1024 * 1024
+HALF_VMEM = 32 * 1024 * 1024
 f32 = jnp.float32
 bf16 = jnp.bfloat16
 i32 = jnp.int32
@@ -269,141 +270,150 @@
         in_specs=[pl.BlockSpec(memory_space=pltpu.SMEM), vmem, vmem, vmem],
         out_specs=(vmem, vmem, vmem, vmem),
         scratch_shapes=[pltpu.VMEM((GX * GY * 8, 128), f32)],
-        compiler_params=pltpu.CompilerParams(vmem_limit_bytes=VMEM_BYTES),
+        compiler_params=pltpu.CompilerParams(vmem_limit_bytes=HALF_VMEM),
         cost_estimate=pl.CostEstimate(flops=10000000000, bytes_accessed=5000000, transcendentals=0),
         name="base_deposit",
     )(base_column, base_zbin, base_frac, base_weight)
 
 
-def halo_kernel(core_ref, front_ref, side_ref, corner_ref, out_ref):
-    out_ref[...] = core_ref[...]
-    out_ref[0, :, :] += front_ref[...]
-    out_ref[:, 0, :] += side_ref[...]
-    out_ref[0, 0:1, :] += corner_ref[...]
+def halo_kernel(core_ref, front_ref, side_ref, corner_ref, out_ref, face_ref, band_ref, sem):
+    slab = pltpu.make_async_copy(core_ref.at[0], face_ref, sem.at[0])
+    band = pltpu.make_async_copy(core_ref.at[pl.ds(1, CX - 1), pl.ds(0, 8), :], band_ref, sem.at[1])
+    slab.start()
+    band.start()
+    slab.wait()
+    face_ref[...] += front_ref[...]
+    face_ref[0:1, :] += side_ref[0:1, :] + corner_ref[...]
+    slab_out = pltpu.make_async_copy(face_ref, out_ref.at[0], sem.at[2])
+    slab_out.start()
+    band.wait()
+    for x in range(1, CX):
+        band_ref[x - 1, 0:1, :] += side_ref[x:x + 1, :]
+    band_out = pltpu.make_async_copy(band_ref, out_ref.at[pl.ds(1, CX - 1), pl.ds(0, 8), :], sem.at[3])
+    band_out.start()
+    slab_out.wait()
+    band_out.wait()
 
 
 def halo_add(core, front, side, corner):
     vmem = pl.BlockSpec(memory_space=pltpu.VMEM)
+    hbm = pl.BlockSpec(memory_space=pltpu.HBM)
     return pl.pallas_call(
         halo_kernel,
         out_shape=jax.ShapeDtypeStruct((CX, CY, NZ), f32),
-        in_specs=[vmem] * 4,
-        out_specs=vmem,
-        compiler_params=pltpu.CompilerParams(vmem_limit_bytes=VMEM_BYTES),
-        cost_estimate=pl.CostEstimate(flops=1000000, bytes_accessed=4500000, transcendentals=0),
+        in_specs=[hbm, vmem, vmem, vmem],
+        out_specs=hbm,
+        input_output_aliases={0: 0},
+        scratch_shapes=[
+            pltpu.VMEM((CY, NZ), f32),
+            pltpu.VMEM((CX - 1, 8, NZ), f32),
+            pltpu.SemaphoreType.DMA((4,)),
+        ],
+        compiler_params=pltpu.CompilerParams(vmem_limit_bytes=HALF_VMEM),
+        cost_estimate=pl.CostEstimate(flops=1000000, bytes_accessed=1500000, transcendentals=0),
         name="halo_add",
     )(core, front, side, corner)
 
 
 ROWS = NODES * SLOTS * 8
 MB = 256
-KB = 512
 
 
 def arrival_rows(heads):
+    count = heads.shape[0]
     line = iota((128, 128), 0)
     lane = iota((128, 128), 1)
     spread = jnp.where(line % 16 == (lane // 8) % 4 * 4 + lane % 4, 1.0, 0.0).astype(bf16)
     labels = (heads + 0.5).astype(i32)
     digits = jnp.concatenate([(labels >> 4).astype(f32), (labels & 15).astype(f32)], axis=0).astype(bf16)
     wide = jnp.dot(digits, spread, preferred_element_type=f32)
-    wide = wide[0:16, :] * 16.0 + wide[16:32, :]
-    wide = jnp.where(iota((16, 128), 0) % 4 == iota((16, 128), 1) // 32, wide, 0.0)
+    wide = wide[0:count, :] * 16.0 + wide[count:2 * count, :]
+    wide = jnp.where(iota((count, 128), 0) % 4 == iota((count, 128), 1) // 32, wide, 0.0)
     shift = 64 * ((iota((1, 128), 1) // 4) % 2)
     return [
-        (jnp.sum(wide[4 * k:4 * k + 4, :], axis=0, keepdims=True) + 0.5).astype(i32) + shift for k in range(4)
+        (jnp.sum(wide[4 * k:4 * k + 4, :], axis=0, keepdims=True) + 0.5).astype(i32) + shift
+        for k in range(count // 4)
     ]
 
 
-def arrival_terms(got_ref):
-    count = got_ref.shape[0]
-    parts = [got_ref[s, :, 0:SLOTS * 1024].reshape(SLOTS * 8, 128) for s in range(count)]
+def one_hot(lines, target):
+    one = jnp.ones(target.shape, bf16)
+    zero = jnp.zeros(target.shape, bf16)
+    return jnp.concatenate(
+        [jnp.where(jnp.broadcast_to(line, target.shape).astype(jnp.int16) == target, one, zero) for line in lines],
+        axis=1,
+    )
+
+
+def arrival_terms(got_ref, first, count):
+    parts = [got_ref[s, :, 0:SLOTS * 1024].reshape(SLOTS * 8, 128) for s in range(first, first + count)]
     high, low = two_terms(jnp.concatenate(parts, axis=0))
-    return high.astype(bf16), low.astype(bf16)
+    return jnp.concatenate([high.astype(bf16), low.astype(bf16)], axis=1)
 
 
 def coarse_kernel(home_ref, got_ref, send_ref, head_ref, sums_ref, part_ref, sem):
-    step = pl.program_id(0)
-    terms = jnp.concatenate(arrival_terms(got_ref), axis=1)
+    terms = arrival_terms(got_ref, 0, NODES)
     lines = []
     for k, row in enumerate(arrival_rows(got_ref[:, 0, SLOTS * 1024:LINE])):
-        head_ref[pl.ds(step * (KB // 128) + k, 1), :] = row
+        head_ref[k:k + 1, :] = row
         lines.append((row >> 10) * 512 + ((row >> 7) & 7) * 64 + (row & 63))
-
-    @pl.when(step == 0)
-    def _():
-        sums_ref[...] = jnp.zeros(sums_ref.shape, f32)
-
     for m in range(1024 // MB):
-        target = iota((MB, 128), 0) + m * MB
-        hot = jnp.concatenate(
-            [jnp.where(jnp.broadcast_to(line, (MB, 128)) == target, 1.0, 0.0).astype(bf16) for line in lines], axis=1
+        target = (iota((MB, 128), 0) + m * MB).astype(jnp.int16)
+        product = jnp.dot(one_hot(lines, target), terms, preferred_element_type=f32)
+        sums_ref[m * MB:(m + 1) * MB, :] = product[:, 0:128] + product[:, 128:256]
+    lane = iota((64, 128), 1)
+    fold_row = iota((512, 128), 0)
+    fold_lane = iota((512, 128), 1)
+    fold = jnp.where((fold_row // 128) * 32 + (fold_row % 64) // 2 == fold_lane, 1.0, 0.0).astype(bf16)
+    for far in (0, 1):
+        pieces = []
+        for q in range(4):
+            spot = (4 * far + q) * 64
+            odd = sums_ref[512 + spot:512 + spot + 64, :]
+            before = jnp.concatenate([jnp.zeros((8, 128), f32), odd[0:56, :]], axis=0)
+            both = sums_ref[spot:spot + 64, :] + jnp.where(lane < 64, odd, before)
+            pieces.append(jnp.concatenate(two_terms(both), axis=0).astype(bf16))
+        folded = jnp.dot(jnp.concatenate(pieces, axis=1), fold, preferred_element_type=f32)
+        part_ref[far * 64:far * 64 + 64, :] = folded[0:64, :] + folded[64:128, :]
+    copies = []
+    for box in range(BPH):
+        for far in (0, 1):
+            hot = part_ref[pl.ds(far * 64 + box, 8, stride=8), :]
+            part_ref[128 + box * 16 + far * 8:128 + box * 16 + far * 8 + 8, :] = hot
+    for box in range(BPH):
+        copy = pltpu.make_async_copy(
+            part_ref.at[pl.ds(128 + box * 16, 16), :], send_ref.at[home_ref[box]], sem.at[box]
         )
-        product = jnp.dot(hot, terms, preferred_element_type=f32)
-        sums_ref[m * MB:(m + 1) * MB, :] += product[:, 0:128] + product[:, 128:256]
-
-    @pl.when(step == ROWS // KB - 1)
-    def _():
-        lane = iota((64, 128), 1)
-        fold_row = iota((512, 128), 0)
-        fold_lane = iota((512, 128), 1)
-        fold = jnp.where((fold_row // 128) * 32 + (fold_row % 64) // 2 == fold_lane, 1.0, 0.0).astype(bf16)
-        for far in (0, 1):
-            pieces = []
-            for q in range(4):
-                spot = (4 * far + q) * 64
-                odd = sums_ref[512 + spot:512 + spot + 64, :]
-                before = jnp.concatenate([jnp.zeros((8, 128), f32), odd[0:56, :]], axis=0)
-                both = sums_ref[spot:spot + 64, :] + jnp.where(lane < 64, odd, before)
-                pieces.append(jnp.concatenate(two_terms(both), axis=0).astype(bf16))
-            folded = jnp.dot(jnp.concatenate(pieces, axis=1), fold, preferred_element_type=f32)
-            part_ref[far * 64:far * 64 + 64, :] = folded[0:64, :] + folded[64:128, :]
-        copies = []
-        for box in range(BPH):
-            for far in (0, 1):
-                hot = part_ref[pl.ds(far * 64 + box, 8, stride=8), :]
-                part_ref[128 + box * 16 + far * 8:128 + box * 16 + far * 8 + 8, :] = hot
-        for box in range(BPH):
-            copy = pltpu.make_async_copy(
-                part_ref.at[pl.ds(128 + box * 16, 16), :], send_ref.at[home_ref[box]], sem.at[box]
-            )
-            copy.start()
-            copies.append(copy)
-        for copy in copies:
-            copy.wait()
+        copy.start()
+        copies.append(copy)
+    for copy in copies:
+        copy.wait()
 
 
 def coarse_deposit(homes, arrived):
+    hbm = pl.BlockSpec(memory_space=pltpu.HBM)
     return pl.pallas_call(
         coarse_kernel,
         out_shape=(jax.ShapeDtypeStruct((NODES, 16, 128), f32), jax.ShapeDtypeStruct((32, 128), i32)),
-        grid=(ROWS // KB,),
-        in_specs=[
-            pl.BlockSpec(memory_space=pltpu.SMEM),
-            pl.BlockSpec((16, 1, LINE), lambda i: (i, 0, 0)),
-        ],
-        out_specs=(pl.BlockSpec(memory_space=pl.ANY), pl.BlockSpec((32, 128), lambda i: (0, 0))),
+        in_specs=[pl.BlockSpec(memory_space=pltpu.SMEM), pl.BlockSpec(memory_space=pltpu.VMEM)],
+        out_specs=(hbm, pl.BlockSpec(memory_space=pltpu.VMEM)),
         scratch_shapes=[
             pltpu.VMEM((1024, 128), f32),
             pltpu.VMEM((256, 128), f32),
             pltpu.SemaphoreType.DMA((BPH,)),
         ],
-        compiler_params=pltpu.CompilerParams(vmem_limit_bytes=VMEM_BYTES),
+        compiler_params=pltpu.CompilerParams(vmem_limit_bytes=HALF_VMEM),
         cost_estimate=pl.CostEstimate(flops=2 * 1024 * ROWS * 256, bytes_accessed=2200000, transcendentals=0),
         name="coarse_deposit",
     )(homes, arrived)
 
 
 def fine_kernel(head_ref, got_ref, fine_ref, terms_ref, sums_ref, hot_ref):
-    high, low = arrival_terms(got_ref)
-    terms_ref[:, 0:128] = high
-    terms_ref[:, 128:256] = low
+    terms_ref[...] = arrival_terms(got_ref, 0, NODES)
 
     def block(m, carry):
-        target = iota((MB, 128), 0) + m * MB
-        for k in range(ROWS // 128):
-            row = jnp.broadcast_to(head_ref[k:k + 1, :], (MB, 128))
-            hot_ref[:, k * 128:k * 128 + 128] = jnp.where(row == target, 1.0, 0.0).astype(bf16)
+        target = (iota((MB, 128), 0) + m * MB).astype(jnp.int16)
+        hot_ref[...] = one_hot([head_ref[k:k + 1, :] for k in range(ROWS // 128)], target)
         product = jnp.dot(hot_ref[...], terms_ref[...], preferred_element_type=f32)
         sums_ref[pl.ds(pl.multiple_of(m * MB, MB), MB), :] = product[:, 0:128] + product[:, 128:256]
         return carry
@@ -431,7 +441,7 @@
             pltpu.VMEM((2048, 128), f32),
             pltpu.VMEM((MB, ROWS), bf16),
         ],
-        compiler_params=pltpu.CompilerParams(vmem_limit_bytes=VMEM_BYTES),
+        compiler_params=pltpu.CompilerParams(vmem_limit_bytes=HALF_VMEM),
         cost_estimate=pl.CostEstimate(flops=2 * 2048 * ROWS * 256, bytes_accessed=4000000, transcendentals=0),
         name="fine_deposit",
     )(header, arrived)
@@ -477,7 +487,7 @@
 
 def lattice_add(owners, places, base, arrived):
     smem = pl.BlockSpec(memory_space=pltpu.SMEM)
-    hbm = pl.BlockSpec(memory_space=pl.ANY)
+    hbm = pl.BlockSpec(memory_space=pltpu.HBM)
     return pl.pallas_call(
         lattice_kernel,
         out_shape=jax.ShapeDtypeStruct((CX, CY, NZ), f32),
@@ -517,16 +527,17 @@
     arrived = lax.all_to_all(outgoing, AXES, split_axis=0, concat_axis=0, tiled=True)
     owners, places = tables(myself.reshape(1), box_home, box_anchor)
     core, front, side, corner = base_deposit(base_column, base_zbin, base_frac, base_weight)
-    front = shifted(front, "blk", 1)
-    side = shifted(side, "cross", 1)
-    corner = diagonal(corner)
     arrived, core, front, side, corner, owners, places = lax.optimization_barrier(
         (arrived, core, front, side, corner, owners, places)
     )
     sending, header = coarse_deposit(homes, arrived)
-    sending, header, core = lax.optimization_barrier((sending, header, core))
+    sending, header, front, side, corner = lax.optimization_barrier((sending, header, front, side, corner))
     returned = lax.all_to_all(sending, AXES, split_axis=0, concat_axis=0, tiled=True)
+    front = shifted(front, "blk", 1)
+    side = shifted(side, "cross", 1)
+    corner = diagonal(corner)
     fine_rows = fine_deposit(header, arrived)
+    front, side, corner, fine_rows = lax.optimization_barrier((front, side, corner, fine_rows))
     base = halo_add(core, front, side, corner)
     returned, base, fine_rows = lax.optimization_barrier((returned, base, fine_rows))
     base_out = lattice_add(owners, places, base, returned)

time: 92 us -> 84.3 us (0.916)
  Pallas kernels: 48.4 us -> 39.4 us
  waiting for transfers between devices: 17.2 us -> 21.5 us
  local copies, waits for them, and re-layouts: 2.33 us -> 0.78 us
  starting transfers between devices: 22.7 us -> 21.4 us
    all_to_all x1, waiting for transfers between devices: 6.08 us -> 15.4 us  [shards(): lax.all_to_all(outgoing, AXES, split_axis=0, concat_axis=0, tiled=True)]
    pallas_call x1, Pallas kernels: 8.96 us -> 4.07 us  [coarse_deposit(): pl.pallas_call(coarse_kernel, out_shape=(jax.ShapeDtypeStruct((NODES, 16,...]
    ppermute x1, waiting for transfers between devices: 3.72 us -> 0.01 us  [diagonal(): return lax.ppermute(value, AXES, pairs)]
    all_to_all x1, waiting for transfers between devices: 7.43 us -> 4.15 us  [shards(): lax.all_to_all(sending, AXES, split_axis=0, concat_axis=0, tiled=True)]
    pallas_call x1, Pallas kernels: 9.12 us -> 6.93 us  [fine_deposit(): pl.pallas_call(fine_kernel, out_shape=jax.ShapeDtypeStruct((BPH, 16384),...]
    ppermute x2, waiting for transfers between devices: 0.01 us -> 1.95 us  [shifted(): return lax.ppermute(value, axis, pairs)]
    pallas_call x1, Pallas kernels: 3.19 us -> 1.79 us  [halo_add(): pl.pallas_call(halo_kernel, out_shape=jax.ShapeDtypeStruct((CX, CY, NZ),...]
    ppermute x1, starting transfers between devices: 1.59 us -> 2.93 us  [diagonal(): return lax.ppermute(value, AXES, pairs)]
  transfers between devices with their start and end apart: 5 -> 5, of which waited for: 3 -> 4; matrix products, arithmetic and copies ran while one was open for 1% -> 1% of each run, Pallas kernels for 31% -> 29%
where the time goes in v2:
time: 84.3 us; the launch traced here: 83.8 us
  Pallas kernels  39.4 us (47%)
  waiting for transfers between devices  21.5 us (26%)
  starting transfers between devices  21.4 us (25%)
    all_to_all x1, waiting for transfers between devices, shards(): lax.all_to_all(outgoing, AXES, split_axis=0, concat_axis=0, tiled=True)  15.4 us
    pallas_call x1, Pallas kernels, base_deposit(): pl.pallas_call(base_kernel, out_shape=(jax.ShapeDtypeStruct((CX, CY, NZ),...  12.4 us
    all_to_all x1, starting transfers between devices, shards(): lax.all_to_all(outgoing, AXES, split_axis=0, concat_axis=0, tiled=True)  11.5 us
    pallas_call x1, Pallas kernels, fine_profiles(): pl.pallas_call(fine_profile_kernel, out_shape=jax.ShapeDtypeStruct((NODES...  8.57 us
    pallas_call x1, Pallas kernels, fine_deposit(): pl.pallas_call(fine_kernel, out_shape=jax.ShapeDtypeStruct((BPH, 16384),...  6.93 us
    all_to_all x1, starting transfers between devices, shards(): lax.all_to_all(sending, AXES, split_axis=0, concat_axis=0, tiled=True)  4.9 us
    all_to_all x1, waiting for transfers between devices, shards(): lax.all_to_all(sending, AXES, split_axis=0, concat_axis=0, tiled=True)  4.15 us
    pallas_call x1, Pallas kernels, coarse_deposit(): pl.pallas_call(coarse_kernel, out_shape=(jax.ShapeDtypeStruct((NODES, 16,...  4.07 us
  transfers between devices with their start and end apart: 5, of which 4 were waited for; matrix products, arithmetic and copies ran while one was open for 1% of the time, Pallas kernels for 29%

profile of v2, /device:TPU:1, one launch (start us, length us, event | category | flops | bytes accessed | tf_op | source)
XLA Modules:
  0.0 83.8 jit_solution(12742048422594589072)
XLA Ops:
  0.6 8.6 %fine_profiles.1 = f32[128,1,4224]{2,1,0:T(1,128)} custom-call(s32[896]{0:T(1024)} %box_ref.1, s32[7,128]{1,0:T(8,128)} %bitcast.4, s32[7,128]{1,0:T(8,128)} %bitcast.5, s32[896,128]{1,0:T(8,128)} %zbin_ref.2, f32[3,896,128]{2,1,0:T(8,128)} %frac_ref.2, f32[896,128]{1,0:T(8,128)} %mass_ref.2), custom_call_target="tpu_custom_call" | custom-call | flops 1879048192 | bytes 4500000 | tf_op jit(solution)/shard_map/fine_profiles/pallas_call | solution.py:156
  9.2 0.0 copy-start
  9.2 0.0 copy-start.1
  9.2 0.0 copy-start.2
  9.2 0.0 copy-start.3
  9.2 11.5 %all-to-all-start = ((f32[128,1,4224]{2,1,0:T(1,128)}), f32[128,1,4224]{2,1,0:T(1,128)S(1)}, u32[]{:S(2)}, u32[]{:S(2)}) async-start(f32[128,1,4224]{2,1,0:T(1,128)} %fine_profiles.1), calls=%async_computation | async-start | bytes 4325376 | tf_op jit(solution)/shard_map/all_to_all | solution.py:527
  20.7 0.8 dynamic_slice.3.home_ref
  21.5 3.0 %tables.1 = (s32[8]{0:T(128)}, s32[8]{0:T(128)}) custom-call(s32[1]{0:T(128)} %bitcast.2.me_ref, s32[8,128]{1,0:T(8,128)} %bitcast.6, s32[1024]{0:T(1024)} %anchor_ref.1), custom_call_target="tpu_custom_call" | custom-call | flops 4000000 | bytes 40000 | tf_op jit(solution)/shard_map/tables/pallas_call | solution.py:199
  24.5 0.0 copy-done
  24.5 0.0 copy-done.1
  24.5 0.0 copy-done.2
  24.5 0.0 copy-done.3
  24.5 12.4 %base_deposit.1 = (f32[8,64,1024]{2,1,0:T(8,128)}, f32[64,1024]{1,0:T(8,128)S(1)}, f32[8,1024]{1,0:T(8,128)S(1)}, f32[1,1024]{1,0:T(1,128)S(1)}) custom-call(s32[256]{0:T(256)S(1)} %copy-done.3, s32[256,128]{1,0:T(8,128)S(1)} %copy-done.1, f32[3,256,128]{2,1,0:T(8,128)S(1)} %copy-done, f32[256,128]{1,0:T(8,128)S(1)} %copy-done.2), custom_call_target="tpu_custom_call" | custom-call | flops 10000000000 | bytes 5000000 | tf_op jit(solution)/shard_map/base_deposit/pallas_call | solution.py:262
  36.9 15.4 %all-to-all-done.got_ref = f32[128,1,4224]{2,1,0:T(1,128)S(1)} async-done(((f32[128,1,4224]{2,1,0:T(1,128)}), f32[128,1,4224]{2,1,0:T(1,128)S(1)}, u32[]{:S(2)}, u32[]{:S(2)}) %all-to-all-start) | async-done | bytes 2162720 | tf_op jit(solution)/shard_map/all_to_all | solution.py:527
  52.3 4.1 %coarse_deposit.1 = (f32[128,16,128]{2,1,0:T(8,128)}, s32[32,128]{1,0:T(8,128)S(1)}) custom-call(s32[8]{0:T(128)S(1)} %dynamic_slice.3.home_ref, f32[128,1,4224]{2,1,0:T(1,128)S(1)} %all-to-all-done.got_ref), custom_call_target="tpu_custom_call" | custom-call | flops 2147483648 | bytes 2200000 | tf_op jit(solution)/shard_map/coarse_deposit/pallas_call | solution.py:395
  56.4 4.9 %all-to-all-start.1 = ((f32[128,16,128]{2,1,0:T(8,128)}), f32[128,16,128]{2,1,0:T(8,128)}, u32[]{:S(2)}, u32[]{:S(2)}) async-start(f32[128,16,128]{2,1,0:T(8,128)} %get-tuple-element.49), calls=%async_computation.1 | async-start | bytes 2097152 | tf_op jit(solution)/shard_map/all_to_all | solution.py:535
  61.3 2.9 %collective-permute-start.2 = (f32[1,1024]{1,0:T(1,128)S(1)}, f32[1,1024]{1,0:T(1,128)S(1)}, u32[]{:S(2)}, u32[]{:S(2)}) collective-permute-start(f32[1,1024]{1,0:T(1,128)S(1)} %get-tuple-element.53), channel_id=1, source_target_pairs={{0,5},{1,6},{2,7},{3,4},{4,9},{5,10},{6,11},{7,8},{8,13},{9,14},{1... | collective-permute-start | bytes 12296 | tf_op jit(solution)/shard_map/ppermute | solution.py:43
  64.2 1.5 %collective-permute-start.1 = (f32[8,1024]{1,0:T(8,128)S(1)}, f32[8,1024]{1,0:T(8,128)S(1)}, u32[]{:S(2)}, u32[]{:S(2)}) collective-permute-start(f32[8,1024]{1,0:T(8,128)S(1)} %get-tuple-element.52), channel_id=1, source_target_pairs={{0,1},{1,2},{2,3},{3,0},{4,5},{5,6},{6,7},{7,4},{8,9},{9,10},{10,1... | collective-permute-start | bytes 98312 | tf_op jit(solution)/shard_map/ppermute | solution.py:33
  65.6 0.6 collective-permute-start
  66.2 6.9 %fine_deposit.1 = f32[8,16384]{1,0:T(8,128)} custom-call(s32[32,128]{1,0:T(8,128)S(1)} %get-tuple-element.54.head_ref, f32[128,1,4224]{2,1,0:T(1,128)S(1)} %all-to-all-done.got_ref), custom_call_target="tpu_custom_call" | custom-call | flops 4294967296 | bytes 4000000 | tf_op jit(solution)/shard_map/fine_deposit/pallas_call | solution.py:434
  73.2 0.0 collective-permute-done.2.corner_ref
  73.2 1.8 %collective-permute-done.1.side_ref = f32[8,1024]{1,0:T(8,128)S(1)} collective-permute-done((f32[8,1024]{1,0:T(8,128)S(1)}, f32[8,1024]{1,0:T(8,128)S(1)}, u32[]{:S(2)}, u32[]{:S(2)}) %collective-permute-start.1) | collective-permute-done | bytes 32800 | tf_op jit(solution)/shard_map/ppermute | solution.py:33
  74.9 0.2 collective-permute-done.front_ref
  75.1 1.8 %halo_add.1.base_ref = f32[8,64,1024]{2,1,0:T(8,128)} custom-call(f32[8,64,1024]{2,1,0:T(8,128)} %get-tuple-element.50.core_ref, f32[64,1024]{1,0:T(8,128)S(1)} %collective-permute-done.front_ref, f32[8,1024]{1,0:T(8,128)S(1)} %collective-permute-done.1.side_ref, f32[1,1024]{1,0:T(1,128)S(1)} %collective-permute-done.2.corner_ref), custom_call_target="tpu_custom_call", output_to_operand_aliasing={{}: (0, {})} | custom-call | flops 1000000 | bytes 1500000 | tf_op jit(solution)/shard_map/halo_add/pallas_call | solution.py:301
  76.9 4.2 %all-to-all-done.1.got_ref = f32[128,16,128]{2,1,0:T(8,128)} async-done(((f32[128,16,128]{2,1,0:T(8,128)}), f32[128,16,128]{2,1,0:T(8,128)}, u32[]{:S(2)}, u32[]{:S(2)}) %all-to-all-start.1) | async-done | bytes 1048608 | tf_op jit(solution)/shard_map/all_to_all | solution.py:535
  81.1 2.7 %lattice_add.1 = f32[8,64,1024]{2,1,0:T(8,128)} custom-call(s32[8]{0:T(128)} %get-tuple-element.41.owner_ref, s32[8]{0:T(128)} %get-tuple-element.42.place_ref, f32[8,64,1024]{2,1,0:T(8,128)} %halo_add.1.base_ref, f32[128,16,128]{2,1,0:T(8,128)} %all-to-all-done.1.got_ref), custom_call_target="tpu_custom_call", output_to_operand_aliasing={{}: (2, {})} | custom-call | flops 1000000 | bytes 1000000 | tf_op jit(solution)/shard_map/lattice_add/pallas_call | solution.py:491
Async XLA Ops:
  9.2 15.3 %copy-start = (f32[3,256,128]{2,1,0:T(8,128)S(1)}, f32[3,256,128]{2,1,0:T(8,128)}, u32[]{:S(2)}) copy-start(f32[3,256,128]{2,1,0:T(8,128)} %frac_ref.3) | copy-start | bytes 1179652
  9.2 15.3 %copy-start.1 = (s32[256,128]{1,0:T(8,128)S(1)}, s32[256,128]{1,0:T(8,128)}, u32[]{:S(2)}) copy-start(s32[256,128]{1,0:T(8,128)} %zbin_ref.3) | copy-start | bytes 393220
  9.2 15.3 %copy-start.2 = (f32[256,128]{1,0:T(8,128)S(1)}, f32[256,128]{1,0:T(8,128)}, u32[]{:S(2)}) copy-start(f32[256,128]{1,0:T(8,128)} %mass_ref.3) | copy-start | bytes 393220
  9.2 15.3 %copy-start.3 = (s32[256]{0:T(256)S(1)}, s32[256]{0:T(256)}, u32[]{:S(2)}) copy-start(s32[256]{0:T(256)} %column_ref) | copy-start | bytes 3076
  9.2 43.0 %all-to-all-start = ((f32[128,1,4224]{2,1,0:T(1,128)}), f32[128,1,4224]{2,1,0:T(1,128)S(1)}, u32[]{:S(2)}, u32[]{:S(2)}) async-start(f32[128,1,4224]{2,1,0:T(1,128)} %fine_profiles.1), calls=%async_computation | async-start | bytes 4325376 | tf_op jit(solution)/shard_map/all_to_all | solution.py:527
  56.4 24.7 %all-to-all-start.1 = ((f32[128,16,128]{2,1,0:T(8,128)}), f32[128,16,128]{2,1,0:T(8,128)}, u32[]{:S(2)}, u32[]{:S(2)}) async-start(f32[128,16,128]{2,1,0:T(8,128)} %get-tuple-element.49), calls=%async_computation.1 | async-start | bytes 2097152 | tf_op jit(solution)/shard_map/all_to_all | solution.py:535
  61.3 11.9 %collective-permute-start.2 = (f32[1,1024]{1,0:T(1,128)S(1)}, f32[1,1024]{1,0:T(1,128)S(1)}, u32[]{:S(2)}, u32[]{:S(2)}) collective-permute-start(f32[1,1024]{1,0:T(1,128)S(1)} %get-tuple-element.53), channel_id=1, source_target_pairs={{0,5},{1,6},{2,7},{3,4},{4,9},{5,10},{6,11},{7,8},{8,13},{9,14},{1... | collective-permute-start | bytes 12296 | tf_op jit(solution)/shard_map/ppermute | solution.py:43
  64.2 10.8 %collective-permute-start.1 = (f32[8,1024]{1,0:T(8,128)S(1)}, f32[8,1024]{1,0:T(8,128)S(1)}, u32[]{:S(2)}, u32[]{:S(2)}) collective-permute-start(f32[8,1024]{1,0:T(8,128)S(1)} %get-tuple-element.52), channel_id=1, source_target_pairs={{0,1},{1,2},{2,3},{3,0},{4,5},{5,6},{6,7},{7,4},{8,9},{9,10},{10,1... | collective-permute-start | bytes 98312 | tf_op jit(solution)/shard_map/ppermute | solution.py:33
  65.6 9.5 %collective-permute-start = (f32[64,1024]{1,0:T(8,128)S(1)}, f32[64,1024]{1,0:T(8,128)S(1)}, u32[]{:S(2)}, u32[]{:S(2)}) collective-permute-start(f32[64,1024]{1,0:T(8,128)S(1)} %get-tuple-element.51), channel_id=1, source_target_pairs={{0,4},{4,8},{8,12},{12,16},{16,20},{20,24},{24,28},{28,32},{32,36}... | collective-permute-start | bytes 786440 | tf_op jit(solution)/shard_map/ppermute | solution.py:33

commit v3 on v2

--- a/solution.py
+++ b/solution.py
@@ -19,8 +19,10 @@
 GY = CY + 1
 AXES = ("blk", "cross")
 PARTS = 4
+ZL = 16
 LINE = SLOTS * 1024 + 128
 VMEM_BYTES = 62 * 1024 * 1024
+ALL_VMEM = 63 * 1024 * 1024 + 512 * 1024
 HALF_VMEM = 32 * 1024 * 1024
 f32 = jnp.float32
 bf16 = jnp.bfloat16
@@ -85,12 +87,12 @@
 
     four_lanes = iota((1, 128), 1) // 4
     sub = iota((8, PT), 0)
-    four = sub % 4
-    turn = (iota((8, PT), 1) // 32 - four) & 3
-    z_row = iota((32, PT), 0).astype(f32).astype(bf16)
-    one = jnp.ones((32, PT), bf16)
-    zero = jnp.zeros((32, PT), bf16)
+    turn = (iota((8, PT), 1) // ZL + sub) & 7
+    z_row = iota((ZL, PT), 0).astype(f32).astype(bf16)
+    one = jnp.ones((ZL, PT), bf16)
+    zero = jnp.zeros((ZL, PT), bf16)
     none = jnp.zeros((16, PT), bf16)
+    uppers = 64 // ZL
 
     def step(i, carry):
         last, head = carry
@@ -101,38 +103,32 @@
         right = []
         for e in (0, 1):
             cell = z + e
-            upper = (cell >> 5).astype(f32)
-            below = jnp.concatenate([upper, upper], axis=0).astype(bf16) == none
+            upper = (cell // ZL).astype(f32)
+            upper = jnp.concatenate([upper, upper], axis=0).astype(bf16)
+            masks = [upper == none + h for h in range(uppers)]
             parts = []
             for a in (0, 1):
                 for b in (0, 1):
                     terms = jnp.concatenate(two_terms(weights[a][b][e]), axis=0).astype(bf16)
-                    parts.append(jnp.where(below, terms, none))
-                    parts.append(jnp.where(below, none, terms))
+                    for mask in masks:
+                        parts.append(jnp.where(mask, terms, none))
             left.append(jnp.concatenate(parts, axis=0))
-            lower = (cell & 31).astype(f32)
+            lower = (cell & (ZL - 1)).astype(f32)
             hots = []
-            for t in range(8):
-                row = jnp.broadcast_to(lower[t:t + 1, :], (32, PT)).astype(bf16)
+            for t in reversed(range(8)):
+                row = jnp.broadcast_to(lower[t:t + 1, :], (ZL, PT)).astype(bf16)
                 hots.append(jnp.where(row == z_row, one, zero))
             right.append(jnp.concatenate(hots, axis=0))
         product = nt_dot(jnp.concatenate(left, axis=1), jnp.concatenate(right, axis=1))
         halves = []
         for a in (0, 1):
-            quarters = []
-            for q in range(4):
-                start = (4 * a + q) * 16
+            gathered = None
+            for q in range(2 * uppers):
+                start = (2 * uppers * a + q) * 16
                 total = product[start:start + 8, :] + product[start + 8:start + 16, :]
-                quarters.append(jnp.where(sub < 4, total[:, 0:128], total[:, 128:256]))
-            gathered = None
-            for s in range(4):
-                value = quarters[s]
-                for k in (1, 2, 3):
-                    value = jnp.where(four == k, quarters[(k + s) % 4], value)
-                if s:
-                    value = pltpu.roll(value, 32 * s, 1)
-                gathered = value if gathered is None else jnp.where(turn == s, value, gathered)
-            halves.append(gathered)
+                value = pltpu.roll(total, ZL * (q + 1), 1) if q < 7 else total
+                gathered = value if gathered is None else jnp.where(turn == q, value, gathered)
+            halves.append(pltpu.roll(gathered, 0, 1, stride=ZL, stride_axis=0))
         first = jnp.where(sub < 4, halves[0], pltpu.roll(halves[1], 4, 0))
         second = jnp.where(sub < 4, pltpu.roll(halves[0], 4, 0), halves[1])
         for g, value in ((0, first), (1, second)):
@@ -241,7 +237,7 @@
                     grid_ref[place, :] += product[start:start + 8, :] + product[start + 8:start + 16, :]
         return carry
 
-    lax.fori_loop(0, BT // 8, step, 0)
+    lax.fori_loop(0, BT // 8, step, 0, unroll=2)
     for x in range(GX):
         for band in range(CY // 8):
             for part in range(8):
@@ -403,7 +399,7 @@
             pltpu.SemaphoreType.DMA((BPH,)),
         ],
         compiler_params=pltpu.CompilerParams(vmem_limit_bytes=HALF_VMEM),
-        cost_estimate=pl.CostEstimate(flops=2 * 1024 * ROWS * 256, bytes_accessed=2200000, transcendentals=0),
+        cost_estimate=pl.CostEstimate(flops=1000, bytes_accessed=1000, transcendentals=0),
         name="coarse_deposit",
     )(homes, arrived)
 
@@ -501,7 +497,7 @@
             pltpu.SemaphoreType.DMA((BPH,)),
             pltpu.SemaphoreType.DMA((BPH,)),
         ],
-        compiler_params=pltpu.CompilerParams(vmem_limit_bytes=VMEM_BYTES),
+        compiler_params=pltpu.CompilerParams(vmem_limit_bytes=ALL_VMEM),
         cost_estimate=pl.CostEstimate(flops=1000000, bytes_accessed=1000000, transcendentals=0),
         name="lattice_add",
     )(owners, places, base, arrived)
@@ -527,17 +523,12 @@
     arrived = lax.all_to_all(outgoing, AXES, split_axis=0, concat_axis=0, tiled=True)
     owners, places = tables(myself.reshape(1), box_home, box_anchor)
     core, front, side, corner = base_deposit(base_column, base_zbin, base_frac, base_weight)
-    arrived, core, front, side, corner, owners, places = lax.optimization_barrier(
-        (arrived, core, front, side, corner, owners, places)
-    )
+    outer = (shifted(front, "blk", 1), shifted(side, "cross", 1), diagonal(corner))
+    arrived, core, owners, places = lax.optimization_barrier((arrived, core, owners, places))
     sending, header = coarse_deposit(homes, arrived)
-    sending, header, front, side, corner = lax.optimization_barrier((sending, header, front, side, corner))
+    sending, header, front, side, corner = lax.optimization_barrier((sending, header, *outer))
     returned = lax.all_to_all(sending, AXES, split_axis=0, concat_axis=0, tiled=True)
-    front = shifted(front, "blk", 1)
-    side = shifted(side, "cross", 1)
-    corner = diagonal(corner)
     fine_rows = fine_deposit(header, arrived)
-    front, side, corner, fine_rows = lax.optimization_barrier((front, side, corner, fine_rows))
     base = halo_add(core, front, side, corner)
     returned, base, fine_rows = lax.optimization_barrier((returned, base, fine_rows))
     base_out = lattice_add(owners, places, base, returned)

time: 84.3 us -> 83.1 us (0.986)
  Pallas kernels: 39.4 us -> 36.7 us
  waiting for transfers between devices: 21.5 us -> 23.7 us
    all_to_all x1, waiting for transfers between devices: 4.15 us -> 10.4 us  [shards(): lax.all_to_all(sending, AXES, split_axis=0, concat_axis=0, tiled=True)]
    all_to_all x1, waiting for transfers between devices: 15.4 us -> 13.3 us  [shards(): lax.all_to_all(outgoing, AXES, split_axis=0, concat_axis=0, tiled=True)]
    pallas_call x1, Pallas kernels: 12.4 us -> 10.3 us  [base_deposit(): pl.pallas_call(base_kernel, out_shape=(jax.ShapeDtypeStruct((CX, CY, NZ),...]
    ppermute x2, waiting for transfers between devices: 1.95 us -> 0.01 us  [shifted(): return lax.ppermute(value, axis, pairs)]
    ppermute x1, starting transfers between devices: 2.93 us -> 1.6 us  [diagonal(): return lax.ppermute(value, AXES, pairs)]
    ppermute x2, starting transfers between devices: 2.05 us -> 3.01 us  [shifted(): return lax.ppermute(value, axis, pairs)]
  transfers between devices with their start and end apart: 5 -> 5, of which waited for: 4 -> 2; matrix products, arithmetic and copies ran while one was open for 1% -> 1% of each run, Pallas kernels for 29% -> 32%
where the time goes in v3:
time: 83.1 us; the launch traced here: 82.7 us
  Pallas kernels  36.7 us (44%)
  waiting for transfers between devices  23.7 us (29%)
  starting transfers between devices  20.8 us (25%)
    all_to_all x1, waiting for transfers between devices, shards(): lax.all_to_all(outgoing, AXES, split_axis=0, concat_axis=0, tiled=True)  13.3 us
    all_to_all x1, starting transfers between devices, shards(): lax.all_to_all(outgoing, AXES, split_axis=0, concat_axis=0, tiled=True)  11.5 us
    all_to_all x1, waiting for transfers between devices, shards(): lax.all_to_all(sending, AXES, split_axis=0, concat_axis=0, tiled=True)  10.4 us
    pallas_call x1, Pallas kernels, base_deposit(): pl.pallas_call(base_kernel, out_shape=(jax.ShapeDtypeStruct((CX, CY, NZ),...  10.3 us
    pallas_call x1, Pallas kernels, fine_profiles(): pl.pallas_call(fine_profile_kernel, out_shape=jax.ShapeDtypeStruct((NODES...  7.92 us
    pallas_call x1, Pallas kernels, fine_deposit(): pl.pallas_call(fine_kernel, out_shape=jax.ShapeDtypeStruct((BPH, 16384),...  6.93 us
    all_to_all x1, starting transfers between devices, shards(): lax.all_to_all(sending, AXES, split_axis=0, concat_axis=0, tiled=True)  4.7 us
    pallas_call x1, Pallas kernels, coarse_deposit(): pl.pallas_call(coarse_kernel, out_shape=(jax.ShapeDtypeStruct((NODES, 16,...  4.09 us
  transfers between devices with their start and end apart: 5, of which 2 were waited for; matrix products, arithmetic and copies ran while one was open for 1% of the time, Pallas kernels for 32%

profile of v3, /device:TPU:1, one launch (start us, length us, event | category | flops | bytes accessed | tf_op | source)
XLA Modules:
  0.0 82.7 jit_solution(17106514406856442347)
XLA Ops:
  0.6 7.9 %fine_profiles.1 = f32[128,1,4224]{2,1,0:T(1,128)} custom-call(s32[896]{0:T(1024)} %box_ref.1, s32[7,128]{1,0:T(8,128)} %bitcast.4, s32[7,128]{1,0:T(8,128)} %bitcast.5, s32[896,128]{1,0:T(8,128)} %zbin_ref.2, f32[3,896,128]{2,1,0:T(8,128)} %frac_ref.2, f32[896,128]{1,0:T(8,128)} %mass_ref.2), custom_call_target="tpu_custom_call" | custom-call | flops 1879048192 | bytes 4500000 | tf_op jit(solution)/shard_map/fine_profiles/pallas_call | solution.py:152
  8.6 0.0 copy-start
  8.6 0.0 copy-start.1
  8.6 0.0 copy-start.2
  8.6 0.0 copy-start.3
  8.6 11.5 %all-to-all-start = ((f32[128,1,4224]{2,1,0:T(1,128)}), f32[128,1,4224]{2,1,0:T(1,128)S(1)}, u32[]{:S(2)}, u32[]{:S(2)}) async-start(f32[128,1,4224]{2,1,0:T(1,128)} %fine_profiles.1), calls=%async_computation | async-start | bytes 4325376 | tf_op jit(solution)/shard_map/all_to_all | solution.py:523
  20.1 0.0 copy-done
  20.1 0.0 copy-done.1
  20.1 0.0 copy-done.2
  20.1 0.0 copy-done.3
  20.1 10.3 %base_deposit.1 = (f32[8,64,1024]{2,1,0:T(8,128)}, f32[64,1024]{1,0:T(8,128)S(1)}, f32[8,1024]{1,0:T(8,128)S(1)}, f32[1,1024]{1,0:T(1,128)S(1)}) custom-call(s32[256]{0:T(256)S(1)} %copy-done.3, s32[256,128]{1,0:T(8,128)S(1)} %copy-done.1, f32[3,256,128]{2,1,0:T(8,128)S(1)} %copy-done, f32[256,128]{1,0:T(8,128)S(1)} %copy-done.2), custom_call_target="tpu_custom_call" | custom-call | flops 10000000000 | bytes 5000000 | tf_op jit(solution)/shard_map/base_deposit/pallas_call | solution.py:258
  30.4 1.6 %collective-permute-start = (f32[64,1024]{1,0:T(8,128)S(1)}, f32[64,1024]{1,0:T(8,128)S(1)}, u32[]{:S(2)}, u32[]{:S(2)}) collective-permute-start(f32[64,1024]{1,0:T(8,128)S(1)} %get-tuple-element.36), channel_id=1, source_target_pairs={{0,4},{4,8},{8,12},{12,16},{16,20},{20,24},{24,28},{28,32},{32,36}... | collective-permute-start | bytes 786440 | tf_op jit(solution)/shard_map/ppermute | solution.py:35
  32.1 1.4 %collective-permute-start.1 = (f32[8,1024]{1,0:T(8,128)S(1)}, f32[8,1024]{1,0:T(8,128)S(1)}, u32[]{:S(2)}, u32[]{:S(2)}) collective-permute-start(f32[8,1024]{1,0:T(8,128)S(1)} %get-tuple-element.37), channel_id=1, source_target_pairs={{0,1},{1,2},{2,3},{3,0},{4,5},{5,6},{6,7},{7,4},{8,9},{9,10},{10,1... | collective-permute-start | bytes 98312 | tf_op jit(solution)/shard_map/ppermute | solution.py:35
  33.4 1.6 %collective-permute-start.2 = (f32[1,1024]{1,0:T(1,128)S(1)}, f32[1,1024]{1,0:T(1,128)S(1)}, u32[]{:S(2)}, u32[]{:S(2)}) collective-permute-start(f32[1,1024]{1,0:T(1,128)S(1)} %get-tuple-element.38), channel_id=1, source_target_pairs={{0,5},{1,6},{2,7},{3,4},{4,9},{5,10},{6,11},{7,8},{8,13},{9,14},{1... | collective-permute-start | bytes 12296 | tf_op jit(solution)/shard_map/ppermute | solution.py:45
  35.0 0.8 dynamic_slice.3.home_ref
  35.8 3.0 %tables.1 = (s32[8]{0:T(128)}, s32[8]{0:T(128)}) custom-call(s32[1]{0:T(128)} %bitcast.2.me_ref, s32[8,128]{1,0:T(8,128)} %bitcast.6, s32[1024]{0:T(1024)} %anchor_ref.1), custom_call_target="tpu_custom_call" | custom-call | flops 4000000 | bytes 40000 | tf_op jit(solution)/shard_map/tables/pallas_call | solution.py:195
  38.8 13.3 %all-to-all-done.got_ref = f32[128,1,4224]{2,1,0:T(1,128)S(1)} async-done(((f32[128,1,4224]{2,1,0:T(1,128)}), f32[128,1,4224]{2,1,0:T(1,128)S(1)}, u32[]{:S(2)}, u32[]{:S(2)}) %all-to-all-start) | async-done | bytes 2162720 | tf_op jit(solution)/shard_map/all_to_all | solution.py:523
  52.0 4.1 %coarse_deposit.1 = (f32[128,16,128]{2,1,0:T(8,128)}, s32[32,128]{1,0:T(8,128)S(1)}) custom-call(s32[8]{0:T(128)S(1)} %dynamic_slice.3.home_ref, f32[128,1,4224]{2,1,0:T(1,128)S(1)} %all-to-all-done.got_ref), custom_call_target="tpu_custom_call" | custom-call | flops 1000 | bytes 1000 | tf_op jit(solution)/shard_map/coarse_deposit/pallas_call | solution.py:391
  56.1 0.0 collective-permute-done.2.corner_ref
  56.1 0.0 collective-permute-done.1.side_ref
  56.2 0.0 collective-permute-done.front_ref
  56.2 4.7 %all-to-all-start.1 = ((f32[128,16,128]{2,1,0:T(8,128)}), f32[128,16,128]{2,1,0:T(8,128)}, u32[]{:S(2)}, u32[]{:S(2)}) async-start(f32[128,16,128]{2,1,0:T(8,128)} %get-tuple-element.39), calls=%async_computation.1 | async-start | bytes 2097152 | tf_op jit(solution)/shard_map/all_to_all | solution.py:530
  60.9 1.8 %halo_add.1.base_ref = f32[8,64,1024]{2,1,0:T(8,128)} custom-call(f32[8,64,1024]{2,1,0:T(8,128)} %get-tuple-element.40.core_ref, f32[64,1024]{1,0:T(8,128)S(1)} %collective-permute-done.front_ref, f32[8,1024]{1,0:T(8,128)S(1)} %collective-permute-done.1.side_ref, f32[1,1024]{1,0:T(1,128)S(1)} %collective-permute-done.2.corner_ref), custom_call_target="tpu_custom_call", output_to_operand_aliasing={{}: (0, {})} | custom-call | flops 1000000 | bytes 1500000 | tf_op jit(solution)/shard_map/halo_add/pallas_call | solution.py:297
  62.7 6.9 %fine_deposit.1 = f32[8,16384]{1,0:T(8,128)} custom-call(s32[32,128]{1,0:T(8,128)S(1)} %get-tuple-element.44.head_ref, f32[128,1,4224]{2,1,0:T(1,128)S(1)} %all-to-all-done.got_ref), custom_call_target="tpu_custom_call" | custom-call | flops 4294967296 | bytes 4000000 | tf_op jit(solution)/shard_map/fine_deposit/pallas_call | solution.py:430
  69.6 10.4 %all-to-all-done.1.got_ref = f32[128,16,128]{2,1,0:T(8,128)} async-done(((f32[128,16,128]{2,1,0:T(8,128)}), f32[128,16,128]{2,1,0:T(8,128)}, u32[]{:S(2)}, u32[]{:S(2)}) %all-to-all-start.1) | async-done | bytes 1048608 | tf_op jit(solution)/shard_map/all_to_all | solution.py:530
  80.0 2.7 %lattice_add.1 = f32[8,64,1024]{2,1,0:T(8,128)} custom-call(s32[8]{0:T(128)} %get-tuple-element.31.owner_ref, s32[8]{0:T(128)} %get-tuple-element.32.place_ref, f32[8,64,1024]{2,1,0:T(8,128)} %halo_add.1.base_ref, f32[128,16,128]{2,1,0:T(8,128)} %all-to-all-done.1.got_ref), custom_call_target="tpu_custom_call", output_to_operand_aliasing={{}: (2, {})} | custom-call | flops 1000000 | bytes 1000000 | tf_op jit(solution)/shard_map/lattice_add/pallas_call | solution.py:487
Async XLA Ops:
  8.6 11.5 %copy-start = (f32[3,256,128]{2,1,0:T(8,128)S(1)}, f32[3,256,128]{2,1,0:T(8,128)}, u32[]{:S(2)}) copy-start(f32[3,256,128]{2,1,0:T(8,128)} %frac_ref.3) | copy-start | bytes 1179652
  8.6 11.5 %copy-start.1 = (s32[256,128]{1,0:T(8,128)S(1)}, s32[256,128]{1,0:T(8,128)}, u32[]{:S(2)}) copy-start(s32[256,128]{1,0:T(8,128)} %zbin_ref.3) | copy-start | bytes 393220
  8.6 11.5 %copy-start.2 = (f32[256,128]{1,0:T(8,128)S(1)}, f32[256,128]{1,0:T(8,128)}, u32[]{:S(2)}) copy-start(f32[256,128]{1,0:T(8,128)} %mass_ref.3) | copy-start | bytes 393220
  8.6 11.5 %copy-start.3 = (s32[256]{0:T(256)S(1)}, s32[256]{0:T(256)}, u32[]{:S(2)}) copy-start(s32[256]{0:T(256)} %column_ref) | copy-start | bytes 3076
  8.6 43.5 %all-to-all-start = ((f32[128,1,4224]{2,1,0:T(1,128)}), f32[128,1,4224]{2,1,0:T(1,128)S(1)}, u32[]{:S(2)}, u32[]{:S(2)}) async-start(f32[128,1,4224]{2,1,0:T(1,128)} %fine_profiles.1), calls=%async_computation | async-start | bytes 4325376 | tf_op jit(solution)/shard_map/all_to_all | solution.py:523
  30.4 25.7 %collective-permute-start = (f32[64,1024]{1,0:T(8,128)S(1)}, f32[64,1024]{1,0:T(8,128)S(1)}, u32[]{:S(2)}, u32[]{:S(2)}) collective-permute-start(f32[64,1024]{1,0:T(8,128)S(1)} %get-tuple-element.36), channel_id=1, source_target_pairs={{0,4},{4,8},{8,12},{12,16},{16,20},{20,24},{24,28},{28,32},{32,36}... | collective-permute-start | bytes 786440 | tf_op jit(solution)/shard_map/ppermute | solution.py:35
  32.1 24.1 %collective-permute-start.1 = (f32[8,1024]{1,0:T(8,128)S(1)}, f32[8,1024]{1,0:T(8,128)S(1)}, u32[]{:S(2)}, u32[]{:S(2)}) collective-permute-start(f32[8,1024]{1,0:T(8,128)S(1)} %get-tuple-element.37), channel_id=1, source_target_pairs={{0,1},{1,2},{2,3},{3,0},{4,5},{5,6},{6,7},{7,4},{8,9},{9,10},{10,1... | collective-permute-start | bytes 98312 | tf_op jit(solution)/shard_map/ppermute | solution.py:35
  33.4 22.7 %collective-permute-start.2 = (f32[1,1024]{1,0:T(1,128)S(1)}, f32[1,1024]{1,0:T(1,128)S(1)}, u32[]{:S(2)}, u32[]{:S(2)}) collective-permute-start(f32[1,1024]{1,0:T(1,128)S(1)} %get-tuple-element.38), channel_id=1, source_target_pairs={{0,5},{1,6},{2,7},{3,4},{4,9},{5,10},{6,11},{7,8},{8,13},{9,14},{1... | collective-permute-start | bytes 12296 | tf_op jit(solution)/shard_map/ppermute | solution.py:45
  56.2 23.9 %all-to-all-start.1 = ((f32[128,16,128]{2,1,0:T(8,128)}), f32[128,16,128]{2,1,0:T(8,128)}, u32[]{:S(2)}, u32[]{:S(2)}) async-start(f32[128,16,128]{2,1,0:T(8,128)} %get-tuple-element.39), calls=%async_computation.1 | async-start | bytes 2097152 | tf_op jit(solution)/shard_map/all_to_all | solution.py:530

commit v4 on v3

--- a/solution.py
+++ b/solution.py
@@ -20,6 +20,7 @@
 AXES = ("blk", "cross")
 PARTS = 4
 ZL = 16
+CHUNKS = 8
 LINE = SLOTS * 1024 + 128
 VMEM_BYTES = 62 * 1024 * 1024
 ALL_VMEM = 63 * 1024 * 1024 + 512 * 1024
@@ -70,7 +71,7 @@
 
 
 def fine_profile_kernel(
-    box_ref, boxes_ref, columns_ref, zbin_ref, frac_ref, mass_ref, out_ref, label_ref, head_ref, last_ref
+    box_ref, boxes_ref, columns_ref, zbin_ref, frac_ref, mass_ref, send_ref, out_ref, label_ref, head_ref, last_ref, sem
 ):
     part = pl.program_id(0)
 
@@ -84,6 +85,7 @@
         label_ref[...] = ((y & 1) * 1024 + (x * 8 + (y >> 1)) * 8 + (boxes & 7)).astype(f32)
         head_ref[...] = jnp.zeros((1, 128), f32)
         last_ref[0] = -1
+        last_ref[1] = 0
 
     four_lanes = iota((1, 128), 1) // 4
     sub = iota((8, PT), 0)
@@ -145,6 +147,23 @@
     last, head = lax.fori_loop(0, steps, step, (last_ref[0], head_ref[...]), unroll=steps)
     last_ref[0] = last
     head_ref[...] = head
+    span = NODES // CHUNKS
+    copies = [
+        pltpu.make_async_copy(out_ref.at[pl.ds(c * span, span)], send_ref.at[pl.ds(c * span, span)], sem.at[c])
+        for c in range(CHUNKS)
+    ]
+    sent = last_ref[1]
+    ready = jnp.where(part == PARTS - 1, CHUNKS, last // span)
+    for c in range(CHUNKS):
+        @pl.when((c >= sent) & (c < ready))
+        def _():
+            copies[c].start()
+    last_ref[1] = ready
+
+    @pl.when(part == PARTS - 1)
+    def _():
+        for copy in copies:
+            copy.wait()
 
 
 def fine_profiles(tile_box, fine_column, fine_zbin, fine_frac, fine_weight):
@@ -161,11 +180,13 @@
             pl.BlockSpec((3, tiles, PT), lambda i: (0, i, 0)),
             pl.BlockSpec((tiles, PT), lambda i: (i, 0)),
         ],
-        out_specs=pl.BlockSpec((NODES, 1, LINE), lambda i: (0, 0, 0)),
+        out_specs=pl.BlockSpec(memory_space=pltpu.HBM),
         scratch_shapes=[
+            pltpu.VMEM((NODES, 1, LINE), f32),
             pltpu.VMEM((FT // 128, 128), f32),
             pltpu.VMEM((1, 128), f32),
-            pltpu.SMEM((1,), i32),
+            pltpu.SMEM((2,), i32),
+            pltpu.SemaphoreType.DMA((CHUNKS,)),
         ],
         compiler_params=pltpu.CompilerParams(vmem_limit_bytes=VMEM_BYTES),
         cost_estimate=pl.CostEstimate(flops=2 * 128 * 256 * 256 * 112, bytes_accessed=4500000, transcendentals=0),

time: 83.1 us -> 82.8 us (level)
  no operation moved by 1% of the time
where the time goes in v4:
time: 82.8 us; the launch traced here: 82.4 us
  Pallas kernels  36.3 us (44%)
  waiting for transfers between devices  23.7 us (29%)
  starting transfers between devices  20.8 us (25%)
    all_to_all x1, waiting for transfers between devices, shards(): lax.all_to_all(outgoing, AXES, split_axis=0, concat_axis=0, tiled=True)  13.3 us
    all_to_all x1, starting transfers between devices, shards(): lax.all_to_all(outgoing, AXES, split_axis=0, concat_axis=0, tiled=True)  11.5 us
    all_to_all x1, waiting for transfers between devices, shards(): lax.all_to_all(sending, AXES, split_axis=0, concat_axis=0, tiled=True)  10.4 us
    pallas_call x1, Pallas kernels, base_deposit(): pl.pallas_call(base_kernel, out_shape=(jax.ShapeDtypeStruct((CX, CY, NZ),...  10.3 us
    pallas_call x1, Pallas kernels, fine_profiles(): pl.pallas_call(fine_profile_kernel, out_shape=jax.ShapeDtypeStruct((NODES...  7.56 us
    pallas_call x1, Pallas kernels, fine_deposit(): pl.pallas_call(fine_kernel, out_shape=jax.ShapeDtypeStruct((BPH, 16384),...  6.93 us
    all_to_all x1, starting transfers between devices, shards(): lax.all_to_all(sending, AXES, split_axis=0, concat_axis=0, tiled=True)  4.7 us
    pallas_call x1, Pallas kernels, coarse_deposit(): pl.pallas_call(coarse_kernel, out_shape=(jax.ShapeDtypeStruct((NODES, 16,...  4.08 us
  transfers between devices with their start and end apart: 5, of which 2 were waited for; matrix products, arithmetic and copies ran while one was open for 1% of the time, Pallas kernels for 32%

profile of v4, /device:TPU:1, one launch (start us, length us, event | category | flops | bytes accessed | tf_op | source)
XLA Modules:
  0.0 82.4 jit_solution(14543806422788117567)
XLA Ops:
  0.6 7.6 %fine_profiles.1 = f32[128,1,4224]{2,1,0:T(1,128)} custom-call(s32[896]{0:T(1024)} %box_ref.1, s32[7,128]{1,0:T(8,128)} %bitcast.4, s32[7,128]{1,0:T(8,128)} %bitcast.5, s32[896,128]{1,0:T(8,128)} %zbin_ref.2, f32[3,896,128]{2,1,0:T(8,128)} %frac_ref.2, f32[896,128]{1,0:T(8,128)} %mass_ref.2), custom_call_target="tpu_custom_call" | custom-call | flops 1879048192 | bytes 4500000 | tf_op jit(solution)/shard_map/fine_profiles/pallas_call | solution.py:171
  8.2 0.0 copy-start
  8.2 0.0 copy-start.1
  8.2 0.0 copy-start.2
  8.2 0.0 copy-start.3
  8.3 11.5 %all-to-all-start = ((f32[128,1,4224]{2,1,0:T(1,128)}), f32[128,1,4224]{2,1,0:T(1,128)S(1)}, u32[]{:S(2)}, u32[]{:S(2)}) async-start(f32[128,1,4224]{2,1,0:T(1,128)} %fine_profiles.1), calls=%async_computation | async-start | bytes 4325376 | tf_op jit(solution)/shard_map/all_to_all | solution.py:544
  19.8 0.0 copy-done
  19.8 0.0 copy-done.1
  19.8 0.0 copy-done.2
  19.8 0.0 copy-done.3
  19.8 10.3 %base_deposit.1 = (f32[8,64,1024]{2,1,0:T(8,128)}, f32[64,1024]{1,0:T(8,128)S(1)}, f32[8,1024]{1,0:T(8,128)S(1)}, f32[1,1024]{1,0:T(1,128)S(1)}) custom-call(s32[256]{0:T(256)S(1)} %copy-done.3, s32[256,128]{1,0:T(8,128)S(1)} %copy-done.1, f32[3,256,128]{2,1,0:T(8,128)S(1)} %copy-done, f32[256,128]{1,0:T(8,128)S(1)} %copy-done.2), custom_call_target="tpu_custom_call" | custom-call | flops 10000000000 | bytes 5000000 | tf_op jit(solution)/shard_map/base_deposit/pallas_call | solution.py:279
  30.1 1.6 %collective-permute-start = (f32[64,1024]{1,0:T(8,128)S(1)}, f32[64,1024]{1,0:T(8,128)S(1)}, u32[]{:S(2)}, u32[]{:S(2)}) collective-permute-start(f32[64,1024]{1,0:T(8,128)S(1)} %get-tuple-element.36), channel_id=1, source_target_pairs={{0,4},{4,8},{8,12},{12,16},{16,20},{20,24},{24,28},{28,32},{32,36}... | collective-permute-start | bytes 786440 | tf_op jit(solution)/shard_map/ppermute | solution.py:36
  31.7 1.4 %collective-permute-start.1 = (f32[8,1024]{1,0:T(8,128)S(1)}, f32[8,1024]{1,0:T(8,128)S(1)}, u32[]{:S(2)}, u32[]{:S(2)}) collective-permute-start(f32[8,1024]{1,0:T(8,128)S(1)} %get-tuple-element.37), channel_id=1, source_target_pairs={{0,1},{1,2},{2,3},{3,0},{4,5},{5,6},{6,7},{7,4},{8,9},{9,10},{10,1... | collective-permute-start | bytes 98312 | tf_op jit(solution)/shard_map/ppermute | solution.py:36
  33.1 1.6 %collective-permute-start.2 = (f32[1,1024]{1,0:T(1,128)S(1)}, f32[1,1024]{1,0:T(1,128)S(1)}, u32[]{:S(2)}, u32[]{:S(2)}) collective-permute-start(f32[1,1024]{1,0:T(1,128)S(1)} %get-tuple-element.38), channel_id=1, source_target_pairs={{0,5},{1,6},{2,7},{3,4},{4,9},{5,10},{6,11},{7,8},{8,13},{9,14},{1... | collective-permute-start | bytes 12296 | tf_op jit(solution)/shard_map/ppermute | solution.py:46
  34.7 0.8 dynamic_slice.3.home_ref
  35.5 3.0 %tables.1 = (s32[8]{0:T(128)}, s32[8]{0:T(128)}) custom-call(s32[1]{0:T(128)} %bitcast.2.me_ref, s32[8,128]{1,0:T(8,128)} %bitcast.6, s32[1024]{0:T(1024)} %anchor_ref.1), custom_call_target="tpu_custom_call" | custom-call | flops 4000000 | bytes 40000 | tf_op jit(solution)/shard_map/tables/pallas_call | solution.py:216
  38.4 13.3 %all-to-all-done.got_ref = f32[128,1,4224]{2,1,0:T(1,128)S(1)} async-done(((f32[128,1,4224]{2,1,0:T(1,128)}), f32[128,1,4224]{2,1,0:T(1,128)S(1)}, u32[]{:S(2)}, u32[]{:S(2)}) %all-to-all-start) | async-done | bytes 2162720 | tf_op jit(solution)/shard_map/all_to_all | solution.py:544
  51.7 4.1 %coarse_deposit.1 = (f32[128,16,128]{2,1,0:T(8,128)}, s32[32,128]{1,0:T(8,128)S(1)}) custom-call(s32[8]{0:T(128)S(1)} %dynamic_slice.3.home_ref, f32[128,1,4224]{2,1,0:T(1,128)S(1)} %all-to-all-done.got_ref), custom_call_target="tpu_custom_call" | custom-call | flops 1000 | bytes 1000 | tf_op jit(solution)/shard_map/coarse_deposit/pallas_call | solution.py:412
  55.8 0.0 collective-permute-done.2.corner_ref
  55.8 0.0 collective-permute-done.1.side_ref
  55.8 0.0 collective-permute-done.front_ref
  55.8 4.7 %all-to-all-start.1 = ((f32[128,16,128]{2,1,0:T(8,128)}), f32[128,16,128]{2,1,0:T(8,128)}, u32[]{:S(2)}, u32[]{:S(2)}) async-start(f32[128,16,128]{2,1,0:T(8,128)} %get-tuple-element.39), calls=%async_computation.1 | async-start | bytes 2097152 | tf_op jit(solution)/shard_map/all_to_all | solution.py:551
  60.6 1.8 %halo_add.1.base_ref = f32[8,64,1024]{2,1,0:T(8,128)} custom-call(f32[8,64,1024]{2,1,0:T(8,128)} %get-tuple-element.40.core_ref, f32[64,1024]{1,0:T(8,128)S(1)} %collective-permute-done.front_ref, f32[8,1024]{1,0:T(8,128)S(1)} %collective-permute-done.1.side_ref, f32[1,1024]{1,0:T(1,128)S(1)} %collective-permute-done.2.corner_ref), custom_call_target="tpu_custom_call", output_to_operand_aliasing={{}: (0, {})} | custom-call | flops 1000000 | bytes 1500000 | tf_op jit(solution)/shard_map/halo_add/pallas_call | solution.py:318
  62.4 6.9 %fine_deposit.1 = f32[8,16384]{1,0:T(8,128)} custom-call(s32[32,128]{1,0:T(8,128)S(1)} %get-tuple-element.44.head_ref, f32[128,1,4224]{2,1,0:T(1,128)S(1)} %all-to-all-done.got_ref), custom_call_target="tpu_custom_call" | custom-call | flops 4294967296 | bytes 4000000 | tf_op jit(solution)/shard_map/fine_deposit/pallas_call | solution.py:451
  69.3 10.4 %all-to-all-done.1.got_ref = f32[128,16,128]{2,1,0:T(8,128)} async-done(((f32[128,16,128]{2,1,0:T(8,128)}), f32[128,16,128]{2,1,0:T(8,128)}, u32[]{:S(2)}, u32[]{:S(2)}) %all-to-all-start.1) | async-done | bytes 1048608 | tf_op jit(solution)/shard_map/all_to_all | solution.py:551
  79.7 2.7 %lattice_add.1 = f32[8,64,1024]{2,1,0:T(8,128)} custom-call(s32[8]{0:T(128)} %get-tuple-element.31.owner_ref, s32[8]{0:T(128)} %get-tuple-element.32.place_ref, f32[8,64,1024]{2,1,0:T(8,128)} %halo_add.1.base_ref, f32[128,16,128]{2,1,0:T(8,128)} %all-to-all-done.1.got_ref), custom_call_target="tpu_custom_call", output_to_operand_aliasing={{}: (2, {})} | custom-call | flops 1000000 | bytes 1000000 | tf_op jit(solution)/shard_map/lattice_add/pallas_call | solution.py:508
Async XLA Ops:
  8.2 11.6 %copy-start = (f32[3,256,128]{2,1,0:T(8,128)S(1)}, f32[3,256,128]{2,1,0:T(8,128)}, u32[]{:S(2)}) copy-start(f32[3,256,128]{2,1,0:T(8,128)} %frac_ref.3) | copy-start | bytes 1179652
  8.2 11.6 %copy-start.1 = (s32[256,128]{1,0:T(8,128)S(1)}, s32[256,128]{1,0:T(8,128)}, u32[]{:S(2)}) copy-start(s32[256,128]{1,0:T(8,128)} %zbin_ref.3) | copy-start | bytes 393220
  8.2 11.6 %copy-start.2 = (f32[256,128]{1,0:T(8,128)S(1)}, f32[256,128]{1,0:T(8,128)}, u32[]{:S(2)}) copy-start(f32[256,128]{1,0:T(8,128)} %mass_ref.3) | copy-start | bytes 393220
  8.2 11.6 %copy-start.3 = (s32[256]{0:T(256)S(1)}, s32[256]{0:T(256)}, u32[]{:S(2)}) copy-start(s32[256]{0:T(256)} %column_ref) | copy-start | bytes 3076
  8.3 43.5 %all-to-all-start = ((f32[128,1,4224]{2,1,0:T(1,128)}), f32[128,1,4224]{2,1,0:T(1,128)S(1)}, u32[]{:S(2)}, u32[]{:S(2)}) async-start(f32[128,1,4224]{2,1,0:T(1,128)} %fine_profiles.1), calls=%async_computation | async-start | bytes 4325376 | tf_op jit(solution)/shard_map/all_to_all | solution.py:544
  30.1 25.7 %collective-permute-start = (f32[64,1024]{1,0:T(8,128)S(1)}, f32[64,1024]{1,0:T(8,128)S(1)}, u32[]{:S(2)}, u32[]{:S(2)}) collective-permute-start(f32[64,1024]{1,0:T(8,128)S(1)} %get-tuple-element.36), channel_id=1, source_target_pairs={{0,4},{4,8},{8,12},{12,16},{16,20},{20,24},{24,28},{28,32},{32,36}... | collective-permute-start | bytes 786440 | tf_op jit(solution)/shard_map/ppermute | solution.py:36
  31.7 24.1 %collective-permute-start.1 = (f32[8,1024]{1,0:T(8,128)S(1)}, f32[8,1024]{1,0:T(8,128)S(1)}, u32[]{:S(2)}, u32[]{:S(2)}) collective-permute-start(f32[8,1024]{1,0:T(8,128)S(1)} %get-tuple-element.37), channel_id=1, source_target_pairs={{0,1},{1,2},{2,3},{3,0},{4,5},{5,6},{6,7},{7,4},{8,9},{9,10},{10,1... | collective-permute-start | bytes 98312 | tf_op jit(solution)/shard_map/ppermute | solution.py:36
  33.1 22.7 %collective-permute-start.2 = (f32[1,1024]{1,0:T(1,128)S(1)}, f32[1,1024]{1,0:T(1,128)S(1)}, u32[]{:S(2)}, u32[]{:S(2)}) collective-permute-start(f32[1,1024]{1,0:T(1,128)S(1)} %get-tuple-element.38), channel_id=1, source_target_pairs={{0,5},{1,6},{2,7},{3,4},{4,9},{5,10},{6,11},{7,8},{8,13},{9,14},{1... | collective-permute-start | bytes 12296 | tf_op jit(solution)/shard_map/ppermute | solution.py:46
  55.8 23.9 %all-to-all-start.1 = ((f32[128,16,128]{2,1,0:T(8,128)}), f32[128,16,128]{2,1,0:T(8,128)}, u32[]{:S(2)}, u32[]{:S(2)}) async-start(f32[128,16,128]{2,1,0:T(8,128)} %get-tuple-element.39), calls=%async_computation.1 | async-start | bytes 2097152 | tf_op jit(solution)/shard_map/all_to_all | solution.py:551

commit v5 on v4

--- a/solution.py
+++ b/solution.py
@@ -369,12 +369,23 @@
 
 
 def coarse_kernel(home_ref, got_ref, send_ref, head_ref, sums_ref, part_ref, sem):
-    terms = arrival_terms(got_ref, 0, NODES)
+    heads = got_ref[:, 0, SLOTS * 1024:LINE]
     lines = []
-    for k, row in enumerate(arrival_rows(got_ref[:, 0, SLOTS * 1024:LINE])):
+    for k, row in enumerate(arrival_rows(heads)):
         head_ref[k:k + 1, :] = row
-        lines.append((row >> 10) * 512 + ((row >> 7) & 7) * 64 + (row & 63))
-    for m in range(1024 // MB):
+        lines.append(((row >> 7) & 7) * 64 + (row & 63))
+    line = iota((32, 128), 0)
+    spots = jnp.where(iota((32, 128), 1) % 16 == line // 8 * 4 + line % 4, 1.0, 0.0).astype(bf16)
+    odd = nt_dot(spots, (((heads + 0.5).astype(i32) >> 10) & 1).astype(f32).astype(bf16))
+    near = iota((32, 128), 1) < 64
+    parts = []
+    for s in range(NODES):
+        value = got_ref[s, :, 0:SLOTS * 1024].reshape(SLOTS * 8, 128)
+        level = jnp.where(near, value + pltpu.roll(value, 64, 1), 0.0)
+        parts.append(jnp.where(jnp.broadcast_to(odd[:, s:s + 1], (32, 128)) > 0.5, value, level))
+    high, low = two_terms(jnp.concatenate(parts, axis=0))
+    terms = jnp.concatenate([high.astype(bf16), low.astype(bf16)], axis=1)
+    for m in range(512 // MB):
         target = (iota((MB, 128), 0) + m * MB).astype(jnp.int16)
         product = jnp.dot(one_hot(lines, target), terms, preferred_element_type=f32)
         sums_ref[m * MB:(m + 1) * MB, :] = product[:, 0:128] + product[:, 128:256]
@@ -386,9 +397,9 @@
         pieces = []
         for q in range(4):
             spot = (4 * far + q) * 64
-            odd = sums_ref[512 + spot:512 + spot + 64, :]
-            before = jnp.concatenate([jnp.zeros((8, 128), f32), odd[0:56, :]], axis=0)
-            both = sums_ref[spot:spot + 64, :] + jnp.where(lane < 64, odd, before)
+            here = sums_ref[spot:spot + 64, :]
+            before = jnp.concatenate([jnp.zeros((8, 128), f32), here[0:56, :]], axis=0)
+            both = jnp.where(lane < 64, here, before)
             pieces.append(jnp.concatenate(two_terms(both), axis=0).astype(bf16))
         folded = jnp.dot(jnp.concatenate(pieces, axis=1), fold, preferred_element_type=f32)
         part_ref[far * 64:far * 64 + 64, :] = folded[0:64, :] + folded[64:128, :]
@@ -415,7 +426,7 @@
         in_specs=[pl.BlockSpec(memory_space=pltpu.SMEM), pl.BlockSpec(memory_space=pltpu.VMEM)],
         out_specs=(hbm, pl.BlockSpec(memory_space=pltpu.VMEM)),
         scratch_shapes=[
-            pltpu.VMEM((1024, 128), f32),
+            pltpu.VMEM((512, 128), f32),
             pltpu.VMEM((256, 128), f32),
             pltpu.SemaphoreType.DMA((BPH,)),
         ],

time: 82.8 us -> 82.3 us (level)
  transfers between devices with their start and end apart: 5 -> 5, of which waited for: 2 -> 2; matrix products, arithmetic and copies ran while one was open for 1% -> 1% of each run, Pallas kernels for 32% -> 31%
where the time goes in v5:
time: 82.3 us; the launch traced here: 81.8 us
  Pallas kernels  35.8 us (43%)
  waiting for transfers between devices  23.7 us (29%)
  starting transfers between devices  20.8 us (25%)
    all_to_all x1, waiting for transfers between devices, shards(): lax.all_to_all(outgoing, AXES, split_axis=0, concat_axis=0, tiled=True)  13.3 us
    all_to_all x1, starting transfers between devices, shards(): lax.all_to_all(outgoing, AXES, split_axis=0, concat_axis=0, tiled=True)  11.5 us
    all_to_all x1, waiting for transfers between devices, shards(): lax.all_to_all(sending, AXES, split_axis=0, concat_axis=0, tiled=True)  10.4 us
    pallas_call x1, Pallas kernels, base_deposit(): pl.pallas_call(base_kernel, out_shape=(jax.ShapeDtypeStruct((CX, CY, NZ),...  10.3 us
    pallas_call x1, Pallas kernels, fine_profiles(): pl.pallas_call(fine_profile_kernel, out_shape=jax.ShapeDtypeStruct((NODES...  7.56 us
    pallas_call x1, Pallas kernels, fine_deposit(): pl.pallas_call(fine_kernel, out_shape=jax.ShapeDtypeStruct((BPH, 16384),...  6.93 us
    all_to_all x1, starting transfers between devices, shards(): lax.all_to_all(sending, AXES, split_axis=0, concat_axis=0, tiled=True)  4.7 us
    pallas_call x1, Pallas kernels, coarse_deposit(): pl.pallas_call(coarse_kernel, out_shape=(jax.ShapeDtypeStruct((NODES, 16,...  3.55 us
  transfers between devices with their start and end apart: 5, of which 2 were waited for; matrix products, arithmetic and copies ran while one was open for 1% of the time, Pallas kernels for 31%

profile of v5, /device:TPU:1, one launch (start us, length us, event | category | flops | bytes accessed | tf_op | source)
XLA Modules:
  0.0 81.8 jit_solution(2372355188751970084)
XLA Ops:
  0.6 7.6 %fine_profiles.1 = f32[128,1,4224]{2,1,0:T(1,128)} custom-call(s32[896]{0:T(1024)} %box_ref.1, s32[7,128]{1,0:T(8,128)} %bitcast.4, s32[7,128]{1,0:T(8,128)} %bitcast.5, s32[896,128]{1,0:T(8,128)} %zbin_ref.2, f32[3,896,128]{2,1,0:T(8,128)} %frac_ref.2, f32[896,128]{1,0:T(8,128)} %mass_ref.2), custom_call_target="tpu_custom_call" | custom-call | flops 1879048192 | bytes 4500000 | tf_op jit(solution)/shard_map/fine_profiles/pallas_call | solution.py:171
  8.2 0.0 copy-start
  8.2 0.0 copy-start.1
  8.2 0.0 copy-start.2
  8.2 0.0 copy-start.3
  8.3 11.5 %all-to-all-start = ((f32[128,1,4224]{2,1,0:T(1,128)}), f32[128,1,4224]{2,1,0:T(1,128)S(1)}, u32[]{:S(2)}, u32[]{:S(2)}) async-start(f32[128,1,4224]{2,1,0:T(1,128)} %fine_profiles.1), calls=%async_computation | async-start | bytes 4325376 | tf_op jit(solution)/shard_map/all_to_all | solution.py:555
  19.8 0.0 copy-done
  19.8 0.0 copy-done.1
  19.8 0.0 copy-done.2
  19.8 0.0 copy-done.3
  19.8 10.3 %base_deposit.1 = (f32[8,64,1024]{2,1,0:T(8,128)}, f32[64,1024]{1,0:T(8,128)S(1)}, f32[8,1024]{1,0:T(8,128)S(1)}, f32[1,1024]{1,0:T(1,128)S(1)}) custom-call(s32[256]{0:T(256)S(1)} %copy-done.3, s32[256,128]{1,0:T(8,128)S(1)} %copy-done.1, f32[3,256,128]{2,1,0:T(8,128)S(1)} %copy-done, f32[256,128]{1,0:T(8,128)S(1)} %copy-done.2), custom_call_target="tpu_custom_call" | custom-call | flops 10000000000 | bytes 5000000 | tf_op jit(solution)/shard_map/base_deposit/pallas_call | solution.py:279
  30.1 1.6 %collective-permute-start = (f32[64,1024]{1,0:T(8,128)S(1)}, f32[64,1024]{1,0:T(8,128)S(1)}, u32[]{:S(2)}, u32[]{:S(2)}) collective-permute-start(f32[64,1024]{1,0:T(8,128)S(1)} %get-tuple-element.36), channel_id=1, source_target_pairs={{0,4},{4,8},{8,12},{12,16},{16,20},{20,24},{24,28},{28,32},{32,36}... | collective-permute-start | bytes 786440 | tf_op jit(solution)/shard_map/ppermute | solution.py:36
  31.7 1.4 %collective-permute-start.1 = (f32[8,1024]{1,0:T(8,128)S(1)}, f32[8,1024]{1,0:T(8,128)S(1)}, u32[]{:S(2)}, u32[]{:S(2)}) collective-permute-start(f32[8,1024]{1,0:T(8,128)S(1)} %get-tuple-element.37), channel_id=1, source_target_pairs={{0,1},{1,2},{2,3},{3,0},{4,5},{5,6},{6,7},{7,4},{8,9},{9,10},{10,1... | collective-permute-start | bytes 98312 | tf_op jit(solution)/shard_map/ppermute | solution.py:36
  33.1 1.6 %collective-permute-start.2 = (f32[1,1024]{1,0:T(1,128)S(1)}, f32[1,1024]{1,0:T(1,128)S(1)}, u32[]{:S(2)}, u32[]{:S(2)}) collective-permute-start(f32[1,1024]{1,0:T(1,128)S(1)} %get-tuple-element.38), channel_id=1, source_target_pairs={{0,5},{1,6},{2,7},{3,4},{4,9},{5,10},{6,11},{7,8},{8,13},{9,14},{1... | collective-permute-start | bytes 12296 | tf_op jit(solution)/shard_map/ppermute | solution.py:46
  34.7 0.8 dynamic_slice.3.home_ref
  35.5 3.0 %tables.1 = (s32[8]{0:T(128)}, s32[8]{0:T(128)}) custom-call(s32[1]{0:T(128)} %bitcast.2.me_ref, s32[8,128]{1,0:T(8,128)} %bitcast.6, s32[1024]{0:T(1024)} %anchor_ref.1), custom_call_target="tpu_custom_call" | custom-call | flops 4000000 | bytes 40000 | tf_op jit(solution)/shard_map/tables/pallas_call | solution.py:216
  38.4 13.3 %all-to-all-done.got_ref = f32[128,1,4224]{2,1,0:T(1,128)S(1)} async-done(((f32[128,1,4224]{2,1,0:T(1,128)}), f32[128,1,4224]{2,1,0:T(1,128)S(1)}, u32[]{:S(2)}, u32[]{:S(2)}) %all-to-all-start) | async-done | bytes 2162720 | tf_op jit(solution)/shard_map/all_to_all | solution.py:555
  51.7 3.6 %coarse_deposit.1 = (f32[128,16,128]{2,1,0:T(8,128)}, s32[32,128]{1,0:T(8,128)S(1)}) custom-call(s32[8]{0:T(128)S(1)} %dynamic_slice.3.home_ref, f32[128,1,4224]{2,1,0:T(1,128)S(1)} %all-to-all-done.got_ref), custom_call_target="tpu_custom_call" | custom-call | flops 1000 | bytes 1000 | tf_op jit(solution)/shard_map/coarse_deposit/pallas_call | solution.py:423
  55.3 0.0 collective-permute-done.2.corner_ref
  55.3 0.0 collective-permute-done.1.side_ref
  55.3 0.0 collective-permute-done.front_ref
  55.3 4.7 %all-to-all-start.1 = ((f32[128,16,128]{2,1,0:T(8,128)}), f32[128,16,128]{2,1,0:T(8,128)}, u32[]{:S(2)}, u32[]{:S(2)}) async-start(f32[128,16,128]{2,1,0:T(8,128)} %get-tuple-element.39), calls=%async_computation.1 | async-start | bytes 2097152 | tf_op jit(solution)/shard_map/all_to_all | solution.py:562
  60.0 1.8 %halo_add.1.base_ref = f32[8,64,1024]{2,1,0:T(8,128)} custom-call(f32[8,64,1024]{2,1,0:T(8,128)} %get-tuple-element.40.core_ref, f32[64,1024]{1,0:T(8,128)S(1)} %collective-permute-done.front_ref, f32[8,1024]{1,0:T(8,128)S(1)} %collective-permute-done.1.side_ref, f32[1,1024]{1,0:T(1,128)S(1)} %collective-permute-done.2.corner_ref), custom_call_target="tpu_custom_call", output_to_operand_aliasing={{}: (0, {})} | custom-call | flops 1000000 | bytes 1500000 | tf_op jit(solution)/shard_map/halo_add/pallas_call | solution.py:318
  61.8 6.9 %fine_deposit.1 = f32[8,16384]{1,0:T(8,128)} custom-call(s32[32,128]{1,0:T(8,128)S(1)} %get-tuple-element.44.head_ref, f32[128,1,4224]{2,1,0:T(1,128)S(1)} %all-to-all-done.got_ref), custom_call_target="tpu_custom_call" | custom-call | flops 4294967296 | bytes 4000000 | tf_op jit(solution)/shard_map/fine_deposit/pallas_call | solution.py:462
  68.8 10.4 %all-to-all-done.1.got_ref = f32[128,16,128]{2,1,0:T(8,128)} async-done(((f32[128,16,128]{2,1,0:T(8,128)}), f32[128,16,128]{2,1,0:T(8,128)}, u32[]{:S(2)}, u32[]{:S(2)}) %all-to-all-start.1) | async-done | bytes 1048608 | tf_op jit(solution)/shard_map/all_to_all | solution.py:562
  79.2 2.7 %lattice_add.1 = f32[8,64,1024]{2,1,0:T(8,128)} custom-call(s32[8]{0:T(128)} %get-tuple-element.31.owner_ref, s32[8]{0:T(128)} %get-tuple-element.32.place_ref, f32[8,64,1024]{2,1,0:T(8,128)} %halo_add.1.base_ref, f32[128,16,128]{2,1,0:T(8,128)} %all-to-all-done.1.got_ref), custom_call_target="tpu_custom_call", output_to_operand_aliasing={{}: (2, {})} | custom-call | flops 1000000 | bytes 1000000 | tf_op jit(solution)/shard_map/lattice_add/pallas_call | solution.py:519
Async XLA Ops:
  8.2 11.6 %copy-start = (f32[3,256,128]{2,1,0:T(8,128)S(1)}, f32[3,256,128]{2,1,0:T(8,128)}, u32[]{:S(2)}) copy-start(f32[3,256,128]{2,1,0:T(8,128)} %frac_ref.3) | copy-start | bytes 1179652
  8.2 11.6 %copy-start.1 = (s32[256,128]{1,0:T(8,128)S(1)}, s32[256,128]{1,0:T(8,128)}, u32[]{:S(2)}) copy-start(s32[256,128]{1,0:T(8,128)} %zbin_ref.3) | copy-start | bytes 393220
  8.2 11.6 %copy-start.2 = (f32[256,128]{1,0:T(8,128)S(1)}, f32[256,128]{1,0:T(8,128)}, u32[]{:S(2)}) copy-start(f32[256,128]{1,0:T(8,128)} %mass_ref.3) | copy-start | bytes 393220
  8.2 11.6 %copy-start.3 = (s32[256]{0:T(256)S(1)}, s32[256]{0:T(256)}, u32[]{:S(2)}) copy-start(s32[256]{0:T(256)} %column_ref) | copy-start | bytes 3076
  8.3 43.5 %all-to-all-start = ((f32[128,1,4224]{2,1,0:T(1,128)}), f32[128,1,4224]{2,1,0:T(1,128)S(1)}, u32[]{:S(2)}, u32[]{:S(2)}) async-start(f32[128,1,4224]{2,1,0:T(1,128)} %fine_profiles.1), calls=%async_computation | async-start | bytes 4325376 | tf_op jit(solution)/shard_map/all_to_all | solution.py:555
  30.1 25.2 %collective-permute-start = (f32[64,1024]{1,0:T(8,128)S(1)}, f32[64,1024]{1,0:T(8,128)S(1)}, u32[]{:S(2)}, u32[]{:S(2)}) collective-permute-start(f32[64,1024]{1,0:T(8,128)S(1)} %get-tuple-element.36), channel_id=1, source_target_pairs={{0,4},{4,8},{8,12},{12,16},{16,20},{20,24},{24,28},{28,32},{32,36}... | collective-permute-start | bytes 786440 | tf_op jit(solution)/shard_map/ppermute | solution.py:36
  31.7 23.6 %collective-permute-start.1 = (f32[8,1024]{1,0:T(8,128)S(1)}, f32[8,1024]{1,0:T(8,128)S(1)}, u32[]{:S(2)}, u32[]{:S(2)}) collective-permute-start(f32[8,1024]{1,0:T(8,128)S(1)} %get-tuple-element.37), channel_id=1, source_target_pairs={{0,1},{1,2},{2,3},{3,0},{4,5},{5,6},{6,7},{7,4},{8,9},{9,10},{10,1... | collective-permute-start | bytes 98312 | tf_op jit(solution)/shard_map/ppermute | solution.py:36
  33.1 22.2 %collective-permute-start.2 = (f32[1,1024]{1,0:T(1,128)S(1)}, f32[1,1024]{1,0:T(1,128)S(1)}, u32[]{:S(2)}, u32[]{:S(2)}) collective-permute-start(f32[1,1024]{1,0:T(1,128)S(1)} %get-tuple-element.38), channel_id=1, source_target_pairs={{0,5},{1,6},{2,7},{3,4},{4,9},{5,10},{6,11},{7,8},{8,13},{9,14},{1... | collective-permute-start | bytes 12296 | tf_op jit(solution)/shard_map/ppermute | solution.py:46
  55.3 23.8 %all-to-all-start.1 = ((f32[128,16,128]{2,1,0:T(8,128)}), f32[128,16,128]{2,1,0:T(8,128)}, u32[]{:S(2)}, u32[]{:S(2)}) async-start(f32[128,16,128]{2,1,0:T(8,128)} %get-tuple-element.39), calls=%async_computation.1 | async-start | bytes 2097152 | tf_op jit(solution)/shard_map/all_to_all | solution.py:562

commit v6 on v5

--- a/solution.py
+++ b/solution.py
@@ -293,7 +293,15 @@
     )(base_column, base_zbin, base_frac, base_weight)
 
 
-def halo_kernel(core_ref, front_ref, side_ref, corner_ref, out_ref, face_ref, band_ref, sem):
+def box_spot(place, grid):
+    rows = pl.ds(pl.multiple_of(((place >> 5) & 7) * 8, 8), 8)
+    lanes = pl.ds(pl.multiple_of(((place >> 2) & 7) * 128, 128), 128)
+    return grid.at[:, rows, lanes]
+
+
+def halo_kernel(
+    place_ref, core_ref, front_ref, side_ref, corner_ref, out_ref, block_ref, face_ref, band_ref, sem, block_sem
+):
     slab = pltpu.make_async_copy(core_ref.at[0], face_ref, sem.at[0])
     band = pltpu.make_async_copy(core_ref.at[pl.ds(1, CX - 1), pl.ds(0, 8), :], band_ref, sem.at[1])
     slab.start()
@@ -310,26 +318,37 @@
     band_out.start()
     slab_out.wait()
     band_out.wait()
-
-
-def halo_add(core, front, side, corner):
+    copies = [
+        pltpu.make_async_copy(box_spot(place_ref[n], out_ref), block_ref.at[n], block_sem.at[n]) for n in range(BPH)
+    ]
+    for copy in copies:
+        copy.start()
+    for copy in copies:
+        copy.wait()
+
+
+def halo_add(places, core, front, side, corner):
     vmem = pl.BlockSpec(memory_space=pltpu.VMEM)
     hbm = pl.BlockSpec(memory_space=pltpu.HBM)
     return pl.pallas_call(
         halo_kernel,
-        out_shape=jax.ShapeDtypeStruct((CX, CY, NZ), f32),
-        in_specs=[hbm, vmem, vmem, vmem],
-        out_specs=hbm,
-        input_output_aliases={0: 0},
+        out_shape=(
+            jax.ShapeDtypeStruct((CX, CY, NZ), f32),
+            jax.ShapeDtypeStruct((BPH, CX, 8, 128), f32),
+        ),
+        in_specs=[pl.BlockSpec(memory_space=pltpu.SMEM), hbm, vmem, vmem, vmem],
+        out_specs=(hbm, hbm),
+        input_output_aliases={1: 0},
         scratch_shapes=[
             pltpu.VMEM((CY, NZ), f32),
             pltpu.VMEM((CX - 1, 8, NZ), f32),
             pltpu.SemaphoreType.DMA((4,)),
+            pltpu.SemaphoreType.DMA((BPH,)),
         ],
         compiler_params=pltpu.CompilerParams(vmem_limit_bytes=HALF_VMEM),
         cost_estimate=pl.CostEstimate(flops=1000000, bytes_accessed=1500000, transcendentals=0),
         name="halo_add",
-    )(core, front, side, corner)
+    )(places, core, front, side, corner)
 
 
 ROWS = NODES * SLOTS * 8
@@ -475,17 +494,11 @@
     )(header, arrived)
 
 
-def lattice_kernel(owner_ref, place_ref, base_ref, got_ref, out_ref, held_ref, block_ref, got_sem, in_sem, out_sem):
-    def spot_of(n, grid):
-        place = place_ref[n]
-        rows = pl.ds(pl.multiple_of(((place >> 5) & 7) * 8, 8), 8)
-        lanes = pl.ds(pl.multiple_of(((place >> 2) & 7) * 128, 128), 128)
-        return grid.at[:, rows, lanes]
-
-    copies = []
-    for n in range(BPH):
-        copies.append(pltpu.make_async_copy(got_ref.at[owner_ref[n]], held_ref.at[n], got_sem.at[n]))
-        copies.append(pltpu.make_async_copy(spot_of(n, base_ref), block_ref.at[n], in_sem.at[n]))
+def lattice_kernel(
+    owner_ref, place_ref, base_ref, blocks_ref, got_ref, out_ref, held_ref, block_ref, got_sem, in_sem, out_sem
+):
+    copies = [pltpu.make_async_copy(got_ref.at[owner_ref[n]], held_ref.at[n], got_sem.at[n]) for n in range(BPH)]
+    copies.append(pltpu.make_async_copy(blocks_ref, block_ref, in_sem.at[0]))
     for copy in copies:
         copy.start()
     firsts = []
@@ -506,33 +519,33 @@
     for n in range(BPH):
         @pl.when(firsts[n] == n)
         def _():
-            pltpu.make_async_copy(block_ref.at[n], spot_of(n, out_ref), out_sem.at[n]).start()
+            pltpu.make_async_copy(block_ref.at[n], box_spot(place_ref[n], out_ref), out_sem.at[n]).start()
     for n in range(BPH):
         @pl.when(firsts[n] == n)
         def _():
-            pltpu.make_async_copy(block_ref.at[n], spot_of(n, out_ref), out_sem.at[n]).wait()
-
-
-def lattice_add(owners, places, base, arrived):
+            pltpu.make_async_copy(block_ref.at[n], box_spot(place_ref[n], out_ref), out_sem.at[n]).wait()
+
+
+def lattice_add(owners, places, base, blocks, arrived):
     smem = pl.BlockSpec(memory_space=pltpu.SMEM)
     hbm = pl.BlockSpec(memory_space=pltpu.HBM)
     return pl.pallas_call(
         lattice_kernel,
         out_shape=jax.ShapeDtypeStruct((CX, CY, NZ), f32),
-        in_specs=[smem, smem, hbm, hbm],
+        in_specs=[smem, smem, hbm, hbm, hbm],
         out_specs=hbm,
         input_output_aliases={2: 0},
         scratch_shapes=[
             pltpu.VMEM((BPH, 16, 128), f32),
             pltpu.VMEM((BPH, CX, 8, 128), f32),
             pltpu.SemaphoreType.DMA((BPH,)),
-            pltpu.SemaphoreType.DMA((BPH,)),
+            pltpu.SemaphoreType.DMA((1,)),
             pltpu.SemaphoreType.DMA((BPH,)),
         ],
         compiler_params=pltpu.CompilerParams(vmem_limit_bytes=ALL_VMEM),
         cost_estimate=pl.CostEstimate(flops=1000000, bytes_accessed=1000000, transcendentals=0),
         name="lattice_add",
-    )(owners, places, base, arrived)
+    )(owners, places, base, blocks, arrived)
 
 
 def shards(
@@ -561,9 +574,9 @@
     sending, header, front, side, corner = lax.optimization_barrier((sending, header, *outer))
     returned = lax.all_to_all(sending, AXES, split_axis=0, concat_axis=0, tiled=True)
     fine_rows = fine_deposit(header, arrived)
-    base = halo_add(core, front, side, corner)
-    returned, base, fine_rows = lax.optimization_barrier((returned, base, fine_rows))
-    base_out = lattice_add(owners, places, base, returned)
+    base, blocks = halo_add(places, core, front, side, corner)
+    returned, base, blocks, fine_rows = lax.optimization_barrier((returned, base, blocks, fine_rows))
+    base_out = lattice_add(owners, places, base, blocks, returned)
     return (base_out, fine_rows)
 
 

time: 82.3 us -> 82.3 us (level)
  waiting for transfers between devices: 23.7 us -> 21.5 us
  Pallas kernels: 35.8 us -> 37.2 us
    all_to_all x1, waiting for transfers between devices: 10.4 us -> 8.2 us  [shards(): lax.all_to_all(sending, AXES, split_axis=0, concat_axis=0, tiled=True)]
    pallas_call x1, Pallas kernels: 1.79 us -> 3.27 us  [halo_add(): pl.pallas_call(halo_kernel, out_shape=(jax.ShapeDtypeStruct((CX, CY, NZ),...]
  transfers between devices with their start and end apart: 5 -> 5, of which waited for: 2 -> 2; matrix products, arithmetic and copies ran while one was open for 1% -> 1% of each run, Pallas kernels for 31% -> 33%
where the time goes in v6:
time: 82.3 us; the launch traced here: 81.8 us
  Pallas kernels  37.2 us (45%)
  waiting for transfers between devices  21.5 us (26%)
  starting transfers between devices  20.8 us (25%)
  local copies, waits for them, and re-layouts  1.5 us (2%)
    all_to_all x1, waiting for transfers between devices, shards(): lax.all_to_all(outgoing, AXES, split_axis=0, concat_axis=0, tiled=True)  13.3 us
    all_to_all x1, starting transfers between devices, shards(): lax.all_to_all(outgoing, AXES, split_axis=0, concat_axis=0, tiled=True)  11.5 us
    pallas_call x1, Pallas kernels, base_deposit(): pl.pallas_call(base_kernel, out_shape=(jax.ShapeDtypeStruct((CX, CY, NZ),...  10.3 us
    all_to_all x1, waiting for transfers between devices, shards(): lax.all_to_all(sending, AXES, split_axis=0, concat_axis=0, tiled=True)  8.2 us
    pallas_call x1, Pallas kernels, fine_profiles(): pl.pallas_call(fine_profile_kernel, out_shape=jax.ShapeDtypeStruct((NODES...  7.48 us
    pallas_call x1, Pallas kernels, fine_deposit(): pl.pallas_call(fine_kernel, out_shape=jax.ShapeDtypeStruct((BPH, 16384),...  6.93 us
    all_to_all x1, starting transfers between devices, shards(): lax.all_to_all(sending, AXES, split_axis=0, concat_axis=0, tiled=True)  4.7 us
    pallas_call x1, Pallas kernels, coarse_deposit(): pl.pallas_call(coarse_kernel, out_shape=(jax.ShapeDtypeStruct((NODES, 16,...  3.56 us
  transfers between devices with their start and end apart: 5, of which 2 were waited for; matrix products, arithmetic and copies ran while one was open for 1% of the time, Pallas kernels for 33%

profile of v6, /device:TPU:1, one launch (start us, length us, event | category | flops | bytes accessed | tf_op | source)
XLA Modules:
  0.0 81.8 jit_solution(16083283059043363279)
XLA Ops:
  0.6 7.5 %fine_profiles.1 = f32[128,1,4224]{2,1,0:T(1,128)} custom-call(s32[896]{0:T(1024)} %box_ref.1, s32[7,128]{1,0:T(8,128)} %bitcast.4, s32[7,128]{1,0:T(8,128)} %bitcast.5, s32[896,128]{1,0:T(8,128)} %zbin_ref.2, f32[3,896,128]{2,1,0:T(8,128)} %frac_ref.2, f32[896,128]{1,0:T(8,128)} %mass_ref.2), custom_call_target="tpu_custom_call" | custom-call | flops 1879048192 | bytes 4500000 | tf_op jit(solution)/shard_map/fine_profiles/pallas_call | solution.py:171
  8.1 0.0 copy-start.2
  8.1 0.0 copy-start.3
  8.2 0.0 copy-start.4
  8.2 0.0 copy-start.5
  8.2 11.5 %all-to-all-start = ((f32[128,1,4224]{2,1,0:T(1,128)}), f32[128,1,4224]{2,1,0:T(1,128)S(1)}, u32[]{:S(2)}, u32[]{:S(2)}) async-start(f32[128,1,4224]{2,1,0:T(1,128)} %fine_profiles.1), calls=%async_computation | async-start | bytes 4325376 | tf_op jit(solution)/shard_map/all_to_all | solution.py:568
  19.7 0.0 copy-done.2
  19.7 0.0 copy-done.3
  19.7 0.0 copy-done.4
  19.7 0.0 copy-done.5
  19.7 10.3 %base_deposit.1 = (f32[8,64,1024]{2,1,0:T(8,128)}, f32[64,1024]{1,0:T(8,128)S(1)}, f32[8,1024]{1,0:T(8,128)S(1)}, f32[1,1024]{1,0:T(1,128)S(1)}) custom-call(s32[256]{0:T(256)S(1)} %copy-done.5, s32[256,128]{1,0:T(8,128)S(1)} %copy-done.3, f32[3,256,128]{2,1,0:T(8,128)S(1)} %copy-done.2, f32[256,128]{1,0:T(8,128)S(1)} %copy-done.4), custom_call_target="tpu_custom_call" | custom-call | flops 10000000000 | bytes 5000000 | tf_op jit(solution)/shard_map/base_deposit/pallas_call | solution.py:279
  30.0 1.6 %collective-permute-start = (f32[64,1024]{1,0:T(8,128)S(1)}, f32[64,1024]{1,0:T(8,128)S(1)}, u32[]{:S(2)}, u32[]{:S(2)}) collective-permute-start(f32[64,1024]{1,0:T(8,128)S(1)} %get-tuple-element.39), channel_id=1, source_target_pairs={{0,4},{4,8},{8,12},{12,16},{16,20},{20,24},{24,28},{28,32},{32,36}... | collective-permute-start | bytes 786440 | tf_op jit(solution)/shard_map/ppermute | solution.py:36
  31.7 1.4 %collective-permute-start.1 = (f32[8,1024]{1,0:T(8,128)S(1)}, f32[8,1024]{1,0:T(8,128)S(1)}, u32[]{:S(2)}, u32[]{:S(2)}) collective-permute-start(f32[8,1024]{1,0:T(8,128)S(1)} %get-tuple-element.40), channel_id=1, source_target_pairs={{0,1},{1,2},{2,3},{3,0},{4,5},{5,6},{6,7},{7,4},{8,9},{9,10},{10,1... | collective-permute-start | bytes 98312 | tf_op jit(solution)/shard_map/ppermute | solution.py:36
  33.0 1.6 %collective-permute-start.2 = (f32[1,1024]{1,0:T(1,128)S(1)}, f32[1,1024]{1,0:T(1,128)S(1)}, u32[]{:S(2)}, u32[]{:S(2)}) collective-permute-start(f32[1,1024]{1,0:T(1,128)S(1)} %get-tuple-element.41), channel_id=1, source_target_pairs={{0,5},{1,6},{2,7},{3,4},{4,9},{5,10},{6,11},{7,8},{8,13},{9,14},{1... | collective-permute-start | bytes 12296 | tf_op jit(solution)/shard_map/ppermute | solution.py:46
  34.6 0.8 dynamic_slice.3.home_ref
  35.4 3.0 %tables.1 = (s32[8]{0:T(128)}, s32[8]{0:T(128)}) custom-call(s32[1]{0:T(128)} %bitcast.2.me_ref, s32[8,128]{1,0:T(8,128)} %bitcast.6, s32[1024]{0:T(1024)} %anchor_ref.1), custom_call_target="tpu_custom_call" | custom-call | flops 4000000 | bytes 40000 | tf_op jit(solution)/shard_map/tables/pallas_call | solution.py:216
  38.4 13.3 %all-to-all-done.got_ref = f32[128,1,4224]{2,1,0:T(1,128)S(1)} async-done(((f32[128,1,4224]{2,1,0:T(1,128)}), f32[128,1,4224]{2,1,0:T(1,128)S(1)}, u32[]{:S(2)}, u32[]{:S(2)}) %all-to-all-start) | async-done | bytes 2162720 | tf_op jit(solution)/shard_map/all_to_all | solution.py:568
  51.6 0.0 copy-start.1
  51.6 3.6 %coarse_deposit.1 = (f32[128,16,128]{2,1,0:T(8,128)}, s32[32,128]{1,0:T(8,128)S(1)}) custom-call(s32[8]{0:T(128)S(1)} %dynamic_slice.3.home_ref, f32[128,1,4224]{2,1,0:T(1,128)S(1)} %all-to-all-done.got_ref), custom_call_target="tpu_custom_call" | custom-call | flops 1000 | bytes 1000 | tf_op jit(solution)/shard_map/coarse_deposit/pallas_call | solution.py:442
  55.2 0.0 collective-permute-done.2.corner_ref
  55.2 0.0 collective-permute-done.1.side_ref
  55.2 0.0 collective-permute-done.front_ref
  55.2 4.7 %all-to-all-start.1 = ((f32[128,16,128]{2,1,0:T(8,128)}), f32[128,16,128]{2,1,0:T(8,128)}, u32[]{:S(2)}, u32[]{:S(2)}) async-start(f32[128,16,128]{2,1,0:T(8,128)} %get-tuple-element.42), calls=%async_computation.1 | async-start | bytes 2097152 | tf_op jit(solution)/shard_map/all_to_all | solution.py:575
  59.9 0.0 copy-done.1
  60.0 3.3 %halo_add.1 = (f32[8,64,1024]{2,1,0:T(8,128)}, f32[8,8,8,128]{3,2,1,0:T(8,128)S(1)}) custom-call(s32[8]{0:T(128)S(1)} %copy-done.1, f32[8,64,1024]{2,1,0:T(8,128)} %get-tuple-element.43.core_ref, f32[64,1024]{1,0:T(8,128)S(1)} %collective-permute-done.front_ref, f32[8,1024]{1,0:T(8,128)S(1)} %collective-permute-done.1.side_ref, ...), custom_call_target="tpu_custom_call", output_to_operand_aliasing={{0}: (1, {})} | custom-call | flops 1000000 | bytes 1500000 | tf_op jit(solution)/shard_map/halo_add/pallas_call | solution.py:333
  63.2 0.0 copy-start
  63.2 0.7 copy-done
  64.0 6.9 %fine_deposit.1 = f32[8,16384]{1,0:T(8,128)} custom-call(s32[32,128]{1,0:T(8,128)S(1)} %get-tuple-element.49.head_ref, f32[128,1,4224]{2,1,0:T(1,128)S(1)} %all-to-all-done.got_ref), custom_call_target="tpu_custom_call" | custom-call | flops 4294967296 | bytes 4000000 | tf_op jit(solution)/shard_map/fine_deposit/pallas_call | solution.py:481
  70.9 8.2 %all-to-all-done.1.got_ref = f32[128,16,128]{2,1,0:T(8,128)} async-done(((f32[128,16,128]{2,1,0:T(8,128)}), f32[128,16,128]{2,1,0:T(8,128)}, u32[]{:S(2)}, u32[]{:S(2)}) %all-to-all-start.1) | async-done | bytes 1048608 | tf_op jit(solution)/shard_map/all_to_all | solution.py:575
  79.1 2.7 %lattice_add.1 = f32[8,64,1024]{2,1,0:T(8,128)} custom-call(s32[8]{0:T(128)} %get-tuple-element.34.owner_ref, s32[8]{0:T(128)} %get-tuple-element.35.place_ref, f32[8,64,1024]{2,1,0:T(8,128)} %get-tuple-element.50.base_ref, f32[8,8,8,128]{3,2,1,0:T(8,128)} %copy-done, f32[128,16,128]{2,1,0:T(8,128)} %all-to-all-done.1.got_ref), custom_call_target="tpu_custom_call", output_to_operand_aliasing={{}: (2, {})} | custom-call | flops 1000000 | bytes 1000000 | tf_op jit(solution)/shard_map/lattice_add/pallas_call | solution.py:532
Async XLA Ops:
  8.1 11.6 %copy-start.2 = (f32[3,256,128]{2,1,0:T(8,128)S(1)}, f32[3,256,128]{2,1,0:T(8,128)}, u32[]{:S(2)}) copy-start(f32[3,256,128]{2,1,0:T(8,128)} %frac_ref.3) | copy-start | bytes 1179652
  8.1 11.6 %copy-start.3 = (s32[256,128]{1,0:T(8,128)S(1)}, s32[256,128]{1,0:T(8,128)}, u32[]{:S(2)}) copy-start(s32[256,128]{1,0:T(8,128)} %zbin_ref.3) | copy-start | bytes 393220
  8.2 11.5 %copy-start.4 = (f32[256,128]{1,0:T(8,128)S(1)}, f32[256,128]{1,0:T(8,128)}, u32[]{:S(2)}) copy-start(f32[256,128]{1,0:T(8,128)} %mass_ref.3) | copy-start | bytes 393220
  8.2 11.5 %copy-start.5 = (s32[256]{0:T(256)S(1)}, s32[256]{0:T(256)}, u32[]{:S(2)}) copy-start(s32[256]{0:T(256)} %column_ref) | copy-start | bytes 3076
  8.2 43.5 %all-to-all-start = ((f32[128,1,4224]{2,1,0:T(1,128)}), f32[128,1,4224]{2,1,0:T(1,128)S(1)}, u32[]{:S(2)}, u32[]{:S(2)}) async-start(f32[128,1,4224]{2,1,0:T(1,128)} %fine_profiles.1), calls=%async_computation | async-start | bytes 4325376 | tf_op jit(solution)/shard_map/all_to_all | solution.py:568
  30.0 25.2 %collective-permute-start = (f32[64,1024]{1,0:T(8,128)S(1)}, f32[64,1024]{1,0:T(8,128)S(1)}, u32[]{:S(2)}, u32[]{:S(2)}) collective-permute-start(f32[64,1024]{1,0:T(8,128)S(1)} %get-tuple-element.39), channel_id=1, source_target_pairs={{0,4},{4,8},{8,12},{12,16},{16,20},{20,24},{24,28},{28,32},{32,36}... | collective-permute-start | bytes 786440 | tf_op jit(solution)/shard_map/ppermute | solution.py:36
  31.7 23.6 %collective-permute-start.1 = (f32[8,1024]{1,0:T(8,128)S(1)}, f32[8,1024]{1,0:T(8,128)S(1)}, u32[]{:S(2)}, u32[]{:S(2)}) collective-permute-start(f32[8,1024]{1,0:T(8,128)S(1)} %get-tuple-element.40), channel_id=1, source_target_pairs={{0,1},{1,2},{2,3},{3,0},{4,5},{5,6},{6,7},{7,4},{8,9},{9,10},{10,1... | collective-permute-start | bytes 98312 | tf_op jit(solution)/shard_map/ppermute | solution.py:36
  33.0 22.2 %collective-permute-start.2 = (f32[1,1024]{1,0:T(1,128)S(1)}, f32[1,1024]{1,0:T(1,128)S(1)}, u32[]{:S(2)}, u32[]{:S(2)}) collective-permute-start(f32[1,1024]{1,0:T(1,128)S(1)} %get-tuple-element.41), channel_id=1, source_target_pairs={{0,5},{1,6},{2,7},{3,4},{4,9},{5,10},{6,11},{7,8},{8,13},{9,14},{1... | collective-permute-start | bytes 12296 | tf_op jit(solution)/shard_map/ppermute | solution.py:46
  51.6 8.3 %copy-start.1 = (s32[8]{0:T(128)S(1)}, s32[8]{0:T(128)}, u32[]{:S(2)}) copy-start(s32[8]{0:T(128)} %get-tuple-element.35.place_ref) | copy-start | bytes 100
  55.2 23.8 %all-to-all-start.1 = ((f32[128,16,128]{2,1,0:T(8,128)}), f32[128,16,128]{2,1,0:T(8,128)}, u32[]{:S(2)}, u32[]{:S(2)}) async-start(f32[128,16,128]{2,1,0:T(8,128)} %get-tuple-element.42), calls=%async_computation.1 | async-start | bytes 2097152 | tf_op jit(solution)/shard_map/all_to_all | solution.py:575
  63.2 0.7 copy-start
